TPU v7x, 256 devices: a whole 4x4x8 slice. The times are simulated.
256 devices in a mesh: ctx: 64 (over x, y_hi, z), resp: 4 (over y_lo, core).
Axes of the slice: x: 4, y: 4 (y_hi: 2, y_lo: 2; y = y_hi * 2 + y_lo), z: 8, core: 2. Of those that a mesh axis runs over, the one named last changes fastest.
Arguments:
- queries: bfloat16 [4, 8192, 2560], P('resp', 'ctx'), may hold values from -30 to 30
- cotangent: bfloat16 [4, 8192, 2560], P('resp', 'ctx'), may hold values from -24 to 24
- sampled_keys: bfloat16 [4, 8192, 512], P('resp', 'ctx'), may hold values from -6 to 6
- sampled_values: bfloat16 [4, 8192, 512], P('resp', 'ctx'), may hold values from -6 to 6
- shared_prompt_keys: bfloat16 [512, 512], P('ctx'), may hold values from -6 to 6
- shared_prompt_values: bfloat16 [512, 512], P('ctx'), may hold values from -6 to 6
- lengths: int32 [4, 8], P('resp'), may hold values from 1 to 2048, 8192 in all within a row
Outputs:
- query_gradient: bfloat16 [4, 8192, 2560], P('resp', 'ctx')
- shared_key_gradient: bfloat16 [512, 512], P('ctx')
- shared_value_gradient: bfloat16 [512, 512], P('ctx')
Inputs may be any that keep to these rules, and one draw needn't show every extreme that they name: Each row holds the lengths of the 8 responses packed one after another into the group's 8192 positions; a row sums to 8192, and its longest response has exactly 2048 positions.
All inputs are finite; a program needn't handle non-finite values.
Results may differ from a plain program's by a relative error of at most 0.0053.
Values may be sent and summed in bfloat16 or wider, within the bound.
A program may use at most 128 MiB of HBM per device.

v0:
```python
import jax
import jax.numpy as jnp
from jax import lax
from jax.sharding import PartitionSpec as P

HEAD_WIDTH = 128
KEY_VALUE_HEADS = 4
QUERY_PER_KEY = 5
HQ = 20


def passed_along(value, axis, by):
    devices = lax.axis_size(axis)
    pairs = [(i, i + by) for i in range(devices) if 0 <= i + by < devices]
    return lax.ppermute(value, axis, pairs)


def row_blocks(row_total):
    return [(0, min(512, row_total))]


def body(
    queries,
    cotangent,
    sampled_keys,
    sampled_values,
    shared_prompt_keys,
    shared_prompt_values,
    lengths,
):
    score_scale = HEAD_WIDTH ** (-0.5)
    count_of_rows = queries.shape[1]
    context_count = lax.axis_size("ctx")
    context_index = lax.axis_index("ctx")
    reach_count = min(16, context_count // 2)
    heads_of_queries = queries[0].reshape(count_of_rows, KEY_VALUE_HEADS, QUERY_PER_KEY, HEAD_WIDTH)
    heads_cotangent = cotangent[0].reshape(
        count_of_rows, KEY_VALUE_HEADS, QUERY_PER_KEY, HEAD_WIDTH
    )
    first_row = context_index * count_of_rows
    query_pos = first_row + jnp.arange(count_of_rows, dtype=jnp.int32)
    segment_ends = jnp.cumsum(lengths[0])

    def segment_of(positions):
        return jnp.sum((segment_ends[None, :] <= positions[:, None]).astype(jnp.int32), axis=1)

    query_segment = segment_of(query_pos)

    def piece_logits(rows_of_keys, rows_of_values, visible):
        heads_of_keys = rows_of_keys.reshape(-1, KEY_VALUE_HEADS, HEAD_WIDTH)
        heads_of_values = rows_of_values.reshape(-1, KEY_VALUE_HEADS, HEAD_WIDTH)
        logits = (
            jnp.einsum(
                "rkqd,jkd->rkqj",
                heads_of_queries,
                heads_of_keys,
                preferred_element_type=jnp.float32,
            )
            * score_scale
        )
        if visible is not None:
            logits = jnp.where(visible[:, None, None, :], logits, -jnp.inf)
        prob_grad = jnp.einsum(
            "rkqd,jkd->rkqj", heads_cotangent, heads_of_values, preferred_element_type=jnp.float32
        )
        return (heads_of_keys, logits, prob_grad)

    def softmax_update(softmax_state, rows_of_keys, rows_of_values, visible):
        top_score, total, weighted = softmax_state
        heads_of_keys, logits, prob_grad = piece_logits(rows_of_keys, rows_of_values, visible)
        new_top = jnp.maximum(top_score, jnp.max(logits, axis=-1))
        factor = jnp.exp(top_score - new_top)
        weights = jnp.exp(logits - new_top[..., None])
        return (
            new_top,
            total * factor + jnp.sum(weights, axis=-1),
            weighted * factor + jnp.sum(weights * prob_grad, axis=-1),
        )

    response_pieces = [(sampled_keys[0], sampled_values[0], 0)]
    for distance in range(1, reach_count + 1):
        earlier_keys, earlier_values = passed_along(
            (sampled_keys[0], sampled_values[0]), "ctx", distance
        )
        response_pieces.append((earlier_keys, earlier_values, distance))

    def piece_visible(distance):
        key_pos = first_row - distance * count_of_rows + jnp.arange(count_of_rows, dtype=jnp.int32)
        key_segment = segment_of(key_pos)
        return (
            (key_pos[None, :] >= 0)
            & (key_pos[None, :] <= query_pos[:, None])
            & (key_segment[None, :] == query_segment[:, None])
        )

    statistic_shape = (count_of_rows, KEY_VALUE_HEADS, QUERY_PER_KEY)
    softmax_state = (
        jnp.full(statistic_shape, -1e30, jnp.float32),
        jnp.zeros(statistic_shape, jnp.float32),
        jnp.zeros(statistic_shape, jnp.float32),
    )
    shard_pair = (
        lax.all_gather(shared_prompt_keys, "ctx", axis=0, tiled=True),
        lax.all_gather(shared_prompt_values, "ctx", axis=0, tiled=True),
    )
    prompt_softmax_state = softmax_state
    prompt_rows_of_keys = shard_pair[0]
    prompt_rows_of_values = shard_pair[1]
    for start, count in row_blocks(prompt_rows_of_keys.shape[0]):
        prompt_softmax_state = softmax_update(
            prompt_softmax_state, prompt_rows_of_keys, prompt_rows_of_values, None
        )
    softmax_state = prompt_softmax_state
    for rows_of_keys, rows_of_values, distance in response_pieces:
        softmax_state = softmax_update(
            softmax_state, rows_of_keys, rows_of_values, piece_visible(distance)
        )
    top_score, total, weighted = softmax_state
    row_delta = weighted / total

    def backward_piece(rows_of_keys, rows_of_values, visible):
        heads_of_keys, logits, prob_grad = piece_logits(rows_of_keys, rows_of_values, visible)
        probs = jnp.exp(logits - top_score[..., None]) / total[..., None]
        logit_grad = score_scale * probs * (prob_grad - row_delta[..., None])
        return (heads_of_keys, probs.astype(jnp.bfloat16), logit_grad.astype(jnp.bfloat16))

    def prompt_update(running, rows_of_keys, rows_of_values):
        query_grad, every_key_gradient, every_value_gradient = running
        for start, count in row_blocks(rows_of_keys.shape[0]):
            heads_of_keys, probs_low, logit_low = backward_piece(rows_of_keys, rows_of_values, None)
            query_grad = jnp.einsum(
                "rkqj,jkd->rkqd", logit_low, heads_of_keys, preferred_element_type=jnp.float32
            )
            key_terms = jnp.einsum(
                "rkqj,rkqd->jkd", logit_low, heads_of_queries, preferred_element_type=jnp.float32
            )
            value_terms = jnp.einsum(
                "rkqj,rkqd->jkd", probs_low, heads_cotangent, preferred_element_type=jnp.float32
            )
            every_key_gradient = key_terms
            every_value_gradient = value_terms
        return (query_grad, every_key_gradient, every_value_gradient)

    prompt_position_total = shared_prompt_keys.shape[0] * context_count
    backward_state = (
        jnp.zeros((count_of_rows, KEY_VALUE_HEADS, QUERY_PER_KEY, HEAD_WIDTH), jnp.float32),
        jnp.zeros((prompt_position_total, KEY_VALUE_HEADS, HEAD_WIDTH), jnp.float32),
        jnp.zeros((prompt_position_total, KEY_VALUE_HEADS, HEAD_WIDTH), jnp.float32),
    )
    shard_pair = (
        lax.all_gather(shared_prompt_keys, "ctx", axis=0, tiled=True),
        lax.all_gather(shared_prompt_values, "ctx", axis=0, tiled=True),
    )
    backward_state = prompt_update(backward_state, shard_pair[0], shard_pair[1])
    query_grad, every_key_gradient, every_value_gradient = backward_state
    for rows_of_keys, rows_of_values, distance in response_pieces:
        response_heads_of_keys, response_probs_low, response_logit_low = backward_piece(
            rows_of_keys, rows_of_values, piece_visible(distance)
        )
        query_grad = query_grad + jnp.einsum(
            "rkqj,jkd->rkqd",
            response_logit_low,
            response_heads_of_keys,
            preferred_element_type=jnp.float32,
        )
    query_gradient = query_grad.astype(jnp.bfloat16).reshape(1, count_of_rows, HQ * HEAD_WIDTH)
    flattened_keys = every_key_gradient.reshape(prompt_position_total, KEY_VALUE_HEADS * HEAD_WIDTH)
    flattened_values = every_value_gradient.reshape(
        prompt_position_total, KEY_VALUE_HEADS * HEAD_WIDTH
    )
    key_part, value_part = (
        lax.psum_scatter(flattened_keys, "ctx", scatter_dimension=0, tiled=True),
        lax.psum_scatter(flattened_values, "ctx", scatter_dimension=0, tiled=True),
    )
    key_whole, value_whole = lax.psum((key_part, value_part), "resp")
    key_out = key_whole.astype(jnp.bfloat16)
    value_out = value_whole.astype(jnp.bfloat16)
    return (query_gradient, key_out, value_out)


def solution(mesh):
    in_specs = (
        P("resp", "ctx", None),
        P("resp", "ctx", None),
        P("resp", "ctx", None),
        P("resp", "ctx", None),
        P("ctx", None),
        P("ctx", None),
        P("resp", None),
    )
    out_specs = (P("resp", "ctx", None), P("ctx", None), P("ctx", None))
    return jax.shard_map(body, mesh=mesh, in_specs=in_specs, out_specs=out_specs, check_vma=False)
```

profile of v0, /device:TPU:1, one launch (start us, length us, event | category | flops | bytes accessed | tf_op | source)
XLA Modules:
  0.0 1293.1 jit_solution(9063679430767620446)
XLA Ops:
  8.9 4.6 collective-permute-start.15
  13.5 10.7 collective-permute-start.14
  24.3 3.4 collective-permute-start.13
  29.4 6.1 collective-permute-start.11
  50.1 150.1 %all_gather.8 = bf16[512,512]{1,0:T(8,128)(2,1)S(1)} all-gather(bf16[8,512]{1,0:T(8,128)(2,1)S(1)} %copy-done.75), channel_id=1, replica_groups=mesh['ctx'=64,'resp'=4] {'ctx'}, dimensions={0}, use_global_device_ids=true | all-gather | bytes 532480 | tf_op jit(solution)/shard_map/all_gather | solution.py:151
  200.8 150.9 %all_gather.9 = bf16[512,512]{1,0:T(8,128)(2,1)S(1)} all-gather(bf16[8,512]{1,0:T(8,128)(2,1)S(1)} %copy-done.76), channel_id=1, replica_groups=mesh['ctx'=64,'resp'=4] {'ctx'}, dimensions={0}, use_global_device_ids=true | all-gather | bytes 532480 | tf_op jit(solution)/shard_map/all_gather | solution.py:152
  367.6 4.2 collective-permute-start.4
  372.1 12.5 collective-permute-start.3
  385.0 11.6 collective-permute-start.2
  398.9 3.0 collective-permute-start
  404.0 5.2 collective-permute-start.30
  409.7 2.2 collective-permute-start.29
  412.3 2.9 collective-permute-start.28
  415.7 2.9 collective-permute-start.27
  423.6 2.2 collective-permute-start.24
  429.9 6.1 collective-permute-start.21
  436.5 5.8 collective-permute-start.20
  443.8 5.6 collective-permute-start.19
  453.6 4.3 collective-permute-start.17
  459.4 3.1 collective-permute-start.16
  474.7 2.3 fusion.7
  477.1 2.6 convolution_bitcast_fusion
  479.6 2.7 fusion.99
  492.6 2.6 copy.393
  495.5 3.3 fusion.94
  498.8 2.6 copy.395
  501.4 3.6 fusion.93
  515.5 2.4 fusion.87
  524.6 3.0 fusion.59
  528.7 334.2 %reduce-scatter.3.cloned.1.call-done = f32[8,512]{1,0:T(8,128)} async-done(((f32[512,512]{1,0:T(8,128)}), f32[8,512]{1,0:T(8,128)}) %reduce-scatter.3.cloned.1.call-update) | async-done | bytes 16400 | tf_op jit(solution)/shard_map/reduce_scatter | solution.py:172
  862.9 359.4 %reduce-scatter.5.cloned.1.call-done = f32[8,512]{1,0:T(8,128)} async-done(((f32[512,512]{1,0:T(8,128)}), f32[8,512]{1,0:T(8,128)}) %reduce-scatter.5.cloned.1.call-update) | async-done | bytes 16400 | tf_op jit(solution)/shard_map/reduce_scatter | solution.py:173
  1222.3 63.9 %all-reduce = (bf16[8,512]{1,0:T(8,128)(2,1)}, bf16[8,512]{1,0:T(8,128)(2,1)}) all-reduce(f32[8,512]{1,0:T(8,128)} %reduce-scatter.3.cloned.1.call-done, f32[8,512]{1,0:T(8,128)} %reduce-scatter.5.cloned.1.call-done), channel_id=1, replica_groups=mesh['ctx'=64,'resp'=4] {'resp'}, use_global_device_ids=true, to_apply=%region_73.74 | all-reduce | flops 8192 | bytes 49152 | tf_op jit(solution)/shard_map/psum | solution.py:175
  (360 shorter events, 97.2 us)
Async XLA Ops:
  7.2 855.7 %reduce-scatter.3.cloned.1.call-start = ((), (), s32[]{:S(2)}) async-start(), calls=%async_computation.2 | async-start | bytes 1064960 | tf_op jit(solution)/shard_map/reduce_scatter | solution.py:172
  8.9 346.5 %collective-permute-start.15 = (bf16[128,512]{0,1:T(8,128)(2,1)}, bf16[128,512]{0,1:T(8,128)(2,1)}, u32[]{:S(2)}, u32[]{:S(2)}) collective-permute-start(bf16[128,512]{0,1:T(8,128)(2,1)} %bitcast.8), channel_id=1, source_target_pairs={{0,64},{4,68},{8,72},{12,76},{16,80},{20,84},{24,88},{28,92},{32,9... | collective-permute-start | bytes 393224 | tf_op jit(solution)/shard_map/ppermute | solution.py:15
  13.5 344.5 %collective-permute-start.14 = (bf16[128,512]{0,1:T(8,128)(2,1)}, bf16[128,512]{0,1:T(8,128)(2,1)}, u32[]{:S(2)}, u32[]{:S(2)}) collective-permute-start(bf16[128,512]{0,1:T(8,128)(2,1)} %bitcast.8), channel_id=1, source_target_pairs={{0,60},{4,64},{8,68},{12,72},{16,76},{20,80},{24,84},{28,88},{32,9... | collective-permute-start | bytes 393224 | tf_op jit(solution)/shard_map/ppermute | solution.py:15
  24.3 336.4 %collective-permute-start.13 = (bf16[128,512]{0,1:T(8,128)(2,1)}, bf16[128,512]{0,1:T(8,128)(2,1)S(1)}, u32[]{:S(2)}, u32[]{:S(2)}) collective-permute-start(bf16[128,512]{0,1:T(8,128)(2,1)} %bitcast.8), channel_id=1, source_target_pairs={{0,56},{4,60},{8,64},{12,68},{16,72},{20,76},{24,80},{28,84},{32,8... | collective-permute-start | bytes 393224 | tf_op jit(solution)/shard_map/ppermute | solution.py:15
  27.6 334.7 %collective-permute-start.12 = (bf16[128,512]{0,1:T(8,128)(2,1)}, bf16[128,512]{0,1:T(8,128)(2,1)S(1)}, u32[]{:S(2)}, u32[]{:S(2)}) collective-permute-start(bf16[128,512]{0,1:T(8,128)(2,1)} %bitcast.8), channel_id=1, source_target_pairs={{0,52},{4,56},{8,60},{12,64},{16,68},{20,72},{24,76},{28,80},{32,8... | collective-permute-start | bytes 393224 | tf_op jit(solution)/shard_map/ppermute | solution.py:15
  29.4 334.7 %collective-permute-start.11 = (bf16[128,512]{0,1:T(8,128)(2,1)}, bf16[128,512]{0,1:T(8,128)(2,1)S(1)}, u32[]{:S(2)}, u32[]{:S(2)}) collective-permute-start(bf16[128,512]{0,1:T(8,128)(2,1)} %bitcast.8), channel_id=1, source_target_pairs={{0,48},{4,52},{8,56},{12,60},{16,64},{20,68},{24,72},{28,76},{32,8... | collective-permute-start | bytes 393224 | tf_op jit(solution)/shard_map/ppermute | solution.py:15
  360.7 11.5 collective-permute-start.8
  362.4 22.6 %collective-permute-start.7 = (bf16[128,512]{0,1:T(8,128)(2,1)}, bf16[128,512]{0,1:T(8,128)(2,1)S(1)}, u32[]{:S(2)}, u32[]{:S(2)}) collective-permute-start(bf16[128,512]{0,1:T(8,128)(2,1)} %bitcast.8), channel_id=1, source_target_pairs={{0,32},{4,36},{8,40},{12,44},{16,48},{20,52},{24,56},{28,60},{32,6... | collective-permute-start | bytes 393224 | tf_op jit(solution)/shard_map/ppermute | solution.py:15
  364.1 33.0 %collective-permute-start.6 = (bf16[128,512]{0,1:T(8,128)(2,1)}, bf16[128,512]{0,1:T(8,128)(2,1)S(1)}, u32[]{:S(2)}, u32[]{:S(2)}) collective-permute-start(bf16[128,512]{0,1:T(8,128)(2,1)} %bitcast.8), channel_id=1, source_target_pairs={{0,28},{4,32},{8,36},{12,40},{16,44},{20,48},{24,52},{28,56},{32,6... | collective-permute-start | bytes 393224 | tf_op jit(solution)/shard_map/ppermute | solution.py:15
  365.8 33.0 %collective-permute-start.5 = (bf16[128,512]{0,1:T(8,128)(2,1)}, bf16[128,512]{0,1:T(8,128)(2,1)S(1)}, u32[]{:S(2)}, u32[]{:S(2)}) collective-permute-start(bf16[128,512]{0,1:T(8,128)(2,1)} %bitcast.8), channel_id=1, source_target_pairs={{0,24},{4,28},{8,32},{12,36},{16,40},{20,44},{24,48},{28,52},{32,5... | collective-permute-start | bytes 393224 | tf_op jit(solution)/shard_map/ppermute | solution.py:15
  367.6 34.7 %collective-permute-start.4 = (bf16[128,512]{0,1:T(8,128)(2,1)}, bf16[128,512]{0,1:T(8,128)(2,1)S(1)}, u32[]{:S(2)}, u32[]{:S(2)}) collective-permute-start(bf16[128,512]{0,1:T(8,128)(2,1)} %bitcast.8), channel_id=1, source_target_pairs={{0,20},{4,24},{8,28},{12,32},{16,36},{20,40},{24,44},{28,48},{32,5... | collective-permute-start | bytes 393224 | tf_op jit(solution)/shard_map/ppermute | solution.py:15
  372.1 31.8 %collective-permute-start.3 = (bf16[128,512]{0,1:T(8,128)(2,1)}, bf16[128,512]{0,1:T(8,128)(2,1)S(1)}, u32[]{:S(2)}, u32[]{:S(2)}) collective-permute-start(bf16[128,512]{0,1:T(8,128)(2,1)} %bitcast.8), channel_id=1, source_target_pairs={{0,16},{4,20},{8,24},{12,28},{16,32},{20,36},{24,40},{28,44},{32,4... | collective-permute-start | bytes 393224 | tf_op jit(solution)/shard_map/ppermute | solution.py:15
  385.0 24.6 %collective-permute-start.2 = (bf16[128,512]{0,1:T(8,128)(2,1)}, bf16[128,512]{0,1:T(8,128)(2,1)S(1)}, u32[]{:S(2)}, u32[]{:S(2)}) collective-permute-start(bf16[128,512]{0,1:T(8,128)(2,1)} %bitcast.8), channel_id=1, source_target_pairs={{0,12},{4,16},{8,20},{12,24},{16,28},{20,32},{24,36},{28,40},{32,4... | collective-permute-start | bytes 393224 | tf_op jit(solution)/shard_map/ppermute | solution.py:15
  397.1 15.2 %collective-permute-start.1 = (bf16[128,512]{0,1:T(8,128)(2,1)}, bf16[128,512]{0,1:T(8,128)(2,1)S(1)}, u32[]{:S(2)}, u32[]{:S(2)}) collective-permute-start(bf16[128,512]{0,1:T(8,128)(2,1)} %bitcast.8), channel_id=1, source_target_pairs={{0,8},{4,12},{8,16},{12,20},{16,24},{20,28},{24,32},{28,36},{32,40... | collective-permute-start | bytes 393224 | tf_op jit(solution)/shard_map/ppermute | solution.py:15
  398.9 16.8 %collective-permute-start = (bf16[128,512]{0,1:T(8,128)(2,1)}, bf16[128,512]{0,1:T(8,128)(2,1)S(1)}, u32[]{:S(2)}, u32[]{:S(2)}) collective-permute-start(bf16[128,512]{0,1:T(8,128)(2,1)} %bitcast.8), channel_id=1, source_target_pairs={{0,4},{4,8},{8,12},{12,16},{16,20},{20,24},{24,28},{28,32},{32,36}... | collective-permute-start | bytes 393224 | tf_op jit(solution)/shard_map/ppermute | solution.py:15
  402.2 16.8 %collective-permute-start.31 = (bf16[128,512]{0,1:T(8,128)(2,1)S(1)}, bf16[128,512]{0,1:T(8,128)(2,1)S(1)}, u32[]{:S(2)}, u32[]{:S(2)}) collective-permute-start(bf16[128,512]{0,1:T(8,128)(2,1)S(1)} %bitcast.548), channel_id=1, source_target_pairs={{0,64},{4,68},{8,72},{12,76},{16,80},{20,84},{24,88},{28,92},{32,9... | collective-permute-start | bytes 393224 | tf_op jit(solution)/shard_map/ppermute | solution.py:15
  404.0 17.5 %collective-permute-start.30 = (bf16[128,512]{0,1:T(8,128)(2,1)S(1)}, bf16[128,512]{0,1:T(8,128)(2,1)S(1)}, u32[]{:S(2)}, u32[]{:S(2)}) collective-permute-start(bf16[128,512]{0,1:T(8,128)(2,1)S(1)} %bitcast.549), channel_id=1, source_target_pairs={{0,60},{4,64},{8,68},{12,72},{16,76},{20,80},{24,84},{28,88},{32,9... | collective-permute-start | bytes 393224 | tf_op jit(solution)/shard_map/ppermute | solution.py:15
  409.7 13.9 %collective-permute-start.29 = (bf16[128,512]{0,1:T(8,128)(2,1)S(1)}, bf16[128,512]{0,1:T(8,128)(2,1)S(1)}, u32[]{:S(2)}, u32[]{:S(2)}) collective-permute-start(bf16[128,512]{0,1:T(8,128)(2,1)S(1)} %bitcast.550), channel_id=1, source_target_pairs={{0,56},{4,60},{8,64},{12,68},{16,72},{20,76},{24,80},{28,84},{32,8... | collective-permute-start | bytes 393224 | tf_op jit(solution)/shard_map/ppermute | solution.py:15
  412.3 14.0 %collective-permute-start.28 = (bf16[128,512]{0,1:T(8,128)(2,1)S(1)}, bf16[128,512]{0,1:T(8,128)(2,1)S(1)}, u32[]{:S(2)}, u32[]{:S(2)}) collective-permute-start(bf16[128,512]{0,1:T(8,128)(2,1)S(1)} %bitcast.551), channel_id=1, source_target_pairs={{0,52},{4,56},{8,60},{12,64},{16,68},{20,72},{24,76},{28,80},{32,8... | collective-permute-start | bytes 393224 | tf_op jit(solution)/shard_map/ppermute | solution.py:15
  415.7 12.5 collective-permute-start.27
  419.0 10.9 collective-permute-start.26
  421.5 15.0 %collective-permute-start.25 = (bf16[128,512]{0,1:T(8,128)(2,1)S(1)}, bf16[128,512]{0,1:T(8,128)(2,1)S(1)}, u32[]{:S(2)}, u32[]{:S(2)}) collective-permute-start(bf16[128,512]{0,1:T(8,128)(2,1)S(1)} %bitcast.554), channel_id=1, source_target_pairs={{0,40},{4,44},{8,48},{12,52},{16,56},{20,60},{24,64},{28,68},{32,7... | collective-permute-start | bytes 393224 | tf_op jit(solution)/shard_map/ppermute | solution.py:15
  423.6 20.2 %collective-permute-start.24 = (bf16[128,512]{0,1:T(8,128)(2,1)S(1)}, bf16[128,512]{0,1:T(8,128)(2,1)S(1)}, u32[]{:S(2)}, u32[]{:S(2)}) collective-permute-start(bf16[128,512]{0,1:T(8,128)(2,1)S(1)} %bitcast.555), channel_id=1, source_target_pairs={{0,36},{4,40},{8,44},{12,48},{16,52},{20,56},{24,60},{28,64},{32,6... | collective-permute-start | bytes 393224 | tf_op jit(solution)/shard_map/ppermute | solution.py:15
  426.3 24.6 %collective-permute-start.23 = (bf16[128,512]{0,1:T(8,128)(2,1)S(1)}, bf16[128,512]{0,1:T(8,128)(2,1)S(1)}, u32[]{:S(2)}, u32[]{:S(2)}) collective-permute-start(bf16[128,512]{0,1:T(8,128)(2,1)S(1)} %bitcast.556), channel_id=1, source_target_pairs={{0,32},{4,36},{8,40},{12,44},{16,48},{20,52},{24,56},{28,60},{32,6... | collective-permute-start | bytes 393224 | tf_op jit(solution)/shard_map/ppermute | solution.py:15
  428.1 25.5 %collective-permute-start.22 = (bf16[128,512]{0,1:T(8,128)(2,1)S(1)}, bf16[128,512]{0,1:T(8,128)(2,1)S(1)}, u32[]{:S(2)}, u32[]{:S(2)}) collective-permute-start(bf16[128,512]{0,1:T(8,128)(2,1)S(1)} %bitcast.557), channel_id=1, source_target_pairs={{0,28},{4,32},{8,36},{12,40},{16,44},{20,48},{24,52},{28,56},{32,6... | collective-permute-start | bytes 393224 | tf_op jit(solution)/shard_map/ppermute | solution.py:15
  429.9 29.6 %collective-permute-start.21 = (bf16[128,512]{0,1:T(8,128)(2,1)S(1)}, bf16[128,512]{0,1:T(8,128)(2,1)S(1)}, u32[]{:S(2)}, u32[]{:S(2)}) collective-permute-start(bf16[128,512]{0,1:T(8,128)(2,1)S(1)} %bitcast.558), channel_id=1, source_target_pairs={{0,24},{4,28},{8,32},{12,36},{16,40},{20,44},{24,48},{28,52},{32,5... | collective-permute-start | bytes 393224 | tf_op jit(solution)/shard_map/ppermute | solution.py:15
  436.5 27.5 %collective-permute-start.20 = (bf16[128,512]{0,1:T(8,128)(2,1)S(1)}, bf16[128,512]{0,1:T(8,128)(2,1)S(1)}, u32[]{:S(2)}, u32[]{:S(2)}) collective-permute-start(bf16[128,512]{0,1:T(8,128)(2,1)S(1)} %bitcast.559), channel_id=1, source_target_pairs={{0,20},{4,24},{8,28},{12,32},{16,36},{20,40},{24,44},{28,48},{32,5... | collective-permute-start | bytes 393224 | tf_op jit(solution)/shard_map/ppermute | solution.py:15
  443.8 21.7 %collective-permute-start.19 = (bf16[128,512]{0,1:T(8,128)(2,1)S(1)}, bf16[128,512]{0,1:T(8,128)(2,1)S(1)}, u32[]{:S(2)}, u32[]{:S(2)}) collective-permute-start(bf16[128,512]{0,1:T(8,128)(2,1)S(1)} %bitcast.560), channel_id=1, source_target_pairs={{0,16},{4,20},{8,24},{12,28},{16,32},{20,36},{24,40},{28,44},{32,4... | collective-permute-start | bytes 393224 | tf_op jit(solution)/shard_map/ppermute | solution.py:15
  450.9 16.0 %collective-permute-start.18 = (bf16[128,512]{0,1:T(8,128)(2,1)S(1)}, bf16[128,512]{0,1:T(8,128)(2,1)S(1)}, u32[]{:S(2)}, u32[]{:S(2)}) collective-permute-start(bf16[128,512]{0,1:T(8,128)(2,1)S(1)} %bitcast.561), channel_id=1, source_target_pairs={{0,12},{4,16},{8,20},{12,24},{16,28},{20,32},{24,36},{28,40},{32,4... | collective-permute-start | bytes 393224 | tf_op jit(solution)/shard_map/ppermute | solution.py:15
  453.6 14.7 %collective-permute-start.17 = (bf16[128,512]{0,1:T(8,128)(2,1)S(1)}, bf16[128,512]{0,1:T(8,128)(2,1)S(1)}, u32[]{:S(2)}, u32[]{:S(2)}) collective-permute-start(bf16[128,512]{0,1:T(8,128)(2,1)S(1)} %bitcast.562), channel_id=1, source_target_pairs={{0,8},{4,12},{8,16},{12,20},{16,24},{20,28},{24,32},{28,36},{32,40... | collective-permute-start | bytes 393224 | tf_op jit(solution)/shard_map/ppermute | solution.py:15
  459.4 10.7 collective-permute-start.16
  495.2 727.1 %reduce-scatter.5.cloned.1.call-start = ((), (), s32[]{:S(2)}) async-start(), calls=%async_computation.3 | async-start | bytes 1064960 | tf_op jit(solution)/shard_map/reduce_scatter | solution.py:173
  (113 other events, 1564.6 us)
Sparse Core Ops, SparseCore 0:
  495.3 367.5 reduce-scatter.2
  865.5 356.7 reduce-scatter.4
where the time goes:
time: 1290 us
  waiting for transfers between devices  694 us (54%)
  blocking collectives  365 us (28%)
  starting transfers between devices  116 us (9%)
  matrix products  67.6 us (5%)
  local copies, waits for them, and re-layouts  20.3 us (2%)
  between operations  16 us (1%)
  other arithmetic  13.9 us (1%)
    reduce_scatter x1, waiting for transfers between devices, body(): lax.psum_scatter(flattened_values, 'ctx', scatter_dimension=0, tiled=True)  359 us
    reduce_scatter x1, waiting for transfers between devices, body(): lax.psum_scatter(flattened_keys, 'ctx', scatter_dimension=0, tiled=True)  334 us
    all_gather x1, blocking collectives, body(): lax.all_gather(shared_prompt_values, 'ctx', axis=0, tiled=True)  151 us
    all_gather x1, blocking collectives, body(): lax.all_gather(shared_prompt_keys, 'ctx', axis=0, tiled=True)  150 us
    ppermute x32, starting transfers between devices, passed_along(): return lax.ppermute(value, axis, pairs)  116 us
    psum x1, blocking collectives, body(): key_whole, value_whole = lax.psum((key_part, value_part), 'resp')  63.9 us
    dot_general x17, matrix products, body(): jnp.einsum('rkqj,jkd->rkqd', response_logit_low, response_heads_of_keys,...  33.3 us
  transfers between devices with their start and end apart: 34, of which 3 were waited for; matrix products, arithmetic and copies ran while one was open for 5% of the time, Pallas kernels for 0%

commit v1 on v0

v1 whole, which is shorter than its diff:
```python
import functools

import jax
import jax.numpy as jnp
from jax import lax
from jax.experimental import pallas as pl
from jax.experimental.pallas import tpu as pltpu
from jax.sharding import PartitionSpec as P

D = 128
KVH = 4
QPK = 5
HQ = KVH * QPK
T = 128
PR = 512
G = QPK * T
NZ = 8
NXY = 8
UP = 4
DOWN = NZ - 1 - UP
SCALE = D ** (-0.5)
LOG2E = 1.4426950408889634
NEG = -1e30
OWN = 16
PROMPT = 17 * T
KEYS = 17 * T + PR
MESH = pl.DeviceIdType.MESH


def remote(src, dst, send, recv, ctx, resp):
    return pltpu.make_async_remote_copy(
        src_ref=src,
        dst_ref=dst,
        send_sem=send,
        recv_sem=recv,
        device_id=(ctx, resp),
        device_id_type=MESH,
    )


def place():
    c = lax.axis_index("ctx")
    r = lax.axis_index("resp")
    z = lax.rem(c, NZ)
    xy = c // NZ
    role = lax.rem(r, 2)
    return c, r, z, xy, role, r + 1 - 2 * role


def greet(peers):
    barrier = pltpu.get_barrier_semaphore()
    for ctx, resp in peers:
        pl.semaphore_signal(barrier, inc=1, device_id=(ctx, resp), device_id_type=MESH)
    pl.semaphore_wait(barrier, len(peers))


class Gather:
    def __init__(self, kv, pg, za, ks, kr, ps, pr):
        self.kv, self.pg, self.za = kv, pg, za
        self.ks, self.kr, self.ps, self.pr = ks, kr, ps, pr
        self.c, self.r, self.z, self.xy, self.role, self.mate = place()

    def peers(self):
        out = []
        for s in range(1, NZ):
            out.append((self.xy * NZ + lax.rem(self.z + s, NZ), self.r))
        for s in range(1, NXY):
            out.append((lax.rem(self.xy + s, NXY) * NZ + self.z, self.r))
        out.append((self.c, self.mate))
        return out

    def piece(self, src, dst, send, ctx):
        return remote(self.kv.at[src], self.kv.at[dst], self.ks.at[send], self.kr.at[dst], ctx, self.r)

    def arrived(self, slot):
        self.piece(slot, slot, slot, self.c).wait_recv()

    def own_sends(self):
        z = self.z
        after = lax.rem(self.c + NZ, NZ * NXY)
        second = lax.rem(self.c + 2 * NZ, NZ * NXY)
        return [
            (None, self.piece(OWN, z, 17, second)),
            (None, self.piece(OWN, 8 + z, 16, after)),
            (z < NZ - 1, self.piece(OWN, z, 18, self.c + 1)),
        ]

    def step(self, s):
        z, c = self.z, self.c
        up = self.xy * NZ + lax.rem(z + 1, NZ)
        down = self.xy * NZ + lax.rem(z + NZ - 1, NZ)
        if s == 0:
            return [
                (None, z, [(z > 0, self.piece(z, z, z, down))]),
                (
                    None,
                    8 + z,
                    [(None, self.piece(8 + z, 8 + z, 19, up)), (None, self.piece(8 + z, 8 + z, 8 + z, down))],
                ),
            ]
        low, high = lax.rem(z - s + NZ, NZ), lax.rem(z + s, NZ)
        out = [
            (z >= s, low, [(z < NZ - 1, self.piece(low, low, low, up))]),
            (z + s < NZ, high, [(z > 0, self.piece(high, high, high, down))]),
        ]
        if s <= UP:
            out.append((None, 8 + low, [(None, self.piece(8 + low, 8 + low, 8 + low, up))] if s < UP else []))
        if s <= DOWN:
            out.append((None, 8 + high, [(None, self.piece(8 + high, 8 + high, 8 + high, down))] if s < DOWN else []))
        return out

    @staticmethod
    def when(condition, do):
        if condition is None:
            do()
        else:
            pl.when(condition)(do)

    def start_own(self):
        for condition, copy in self.own_sends():
            self.when(condition, copy.start)

    def take_step(self, s):
        for condition, slot, sends in self.step(s):

            def take(slot=slot, sends=sends):
                self.arrived(slot)
                for inner, copy in sends:
                    self.when(inner, copy.start)

            self.when(condition, take)

    def finish(self):
        for condition, copy in self.own_sends():
            self.when(condition, copy.wait_send)
        for s in range(NZ):
            for condition, slot, sends in self.step(s):

                def done(sends=sends):
                    for inner, copy in sends:
                        self.when(inner, copy.wait_send)

                self.when(condition, done)

    def prompt_z(self, pk, pv):
        z = self.z
        mine = jnp.where(self.role == 0, pk[...].astype(jnp.float32), pv[...].astype(jnp.float32))
        self.za[z] = mine
        self.zcopies = [
            remote(
                self.za.at[z],
                self.za.at[z],
                self.ps.at[s],
                self.pr.at[s],
                self.xy * NZ + lax.rem(z + s, NZ),
                self.r,
            )
            for s in range(1, NZ)
        ]
        for copy in self.zcopies:
            copy.start()

    def prompt_xy(self):
        for s, copy in enumerate(self.zcopies, 1):
            source = lax.rem(self.z - s + NZ, NZ)
            remote(self.za.at[source], self.za.at[source], self.ps.at[s], self.pr.at[s], self.c, self.r).wait_recv()
        rows = pl.ds(pl.multiple_of(self.xy * 64, 64), 64)
        self.pg[self.role, rows, :] = self.za[...].reshape(64, 512).astype(jnp.bfloat16)
        self.xycopies = [
            remote(
                self.pg.at[self.role, rows],
                self.pg.at[self.role, rows],
                self.ps.at[8 + s],
                self.pr.at[8 + s],
                lax.rem(self.xy + s, NXY) * NZ + self.z,
                self.r,
            )
            for s in range(1, NXY)
        ]
        for copy in self.xycopies:
            copy.start()

    def prompt_core(self):
        for s in range(1, NXY):
            source = lax.rem(self.xy - s + NXY, NXY)
            rows = pl.ds(pl.multiple_of(source * 64, 64), 64)
            block = self.pg.at[self.role, rows]
            remote(block, block, self.ps.at[8 + s], self.pr.at[8 + s], self.c, self.r).wait_recv()
        half = self.pg.at[self.role]
        self.corecopy = remote(half, half, self.ps.at[0], self.pr.at[0], self.c, self.mate)
        self.corecopy.start()

    def prompt_done(self):
        other = self.pg.at[1 - self.role]
        remote(other, other, self.ps.at[0], self.pr.at[0], self.c, self.mate).wait_recv()
        for copy in self.zcopies + self.xycopies + [self.corecopy]:
            copy.wait_send()


def gather_kernel(k, v, pk, pv, kv, pg, za, ks, kr, ps, pr):
    g = Gather(kv, pg, za, ks, kr, ps, pr)
    kv[OWN, :, :512] = k[...]
    kv[OWN, :, 512:] = v[...]
    greet(g.peers())
    g.prompt_z(pk, pv)
    g.start_own()
    g.prompt_xy()
    g.take_step(0)
    g.prompt_core()
    for s in range(1, NZ):
        g.take_step(s)
    g.prompt_done()
    g.finish()


class Attend:
    def __init__(self, q, do, kv, pg, lengths, sc):
        self.q, self.do, self.kv, self.pg, self.lengths = q, do, kv, pg, lengths
        (self.qt, self.dot_, self.qn, self.don, self.e, self.dp, self.m, self.l, self.w, self.mb, self.dq) = sc

    def prepare(self):
        for k in range(KVH):
            for h in range(QPK):
                cols = slice((k * QPK + h) * D, (k * QPK + h + 1) * D)
                rows = slice(h * T, (h + 1) * T)
                self.qn[k, rows, :] = self.q[:, cols]
                self.don[k, rows, :] = self.do[:, cols]
                self.qt[k, :, rows] = self.q[:, cols].T
                self.dot_[k, :, rows] = self.do[:, cols].T
        self.m[...] = jnp.full(self.m.shape, NEG, jnp.float32)
        self.l[...] = jnp.zeros(self.l.shape, jnp.float32)
        self.w[...] = jnp.zeros(self.w.shape, jnp.float32)
        self.dq[...] = jnp.zeros(self.dq.shape, jnp.float32)
        c = lax.axis_index("ctx")
        self.first = c * T
        self.qpos = self.first + lax.broadcasted_iota(jnp.int32, (1, T), 1)
        start = jnp.zeros((1, T), jnp.int32)
        end = jnp.int32(0)
        for s in range(8):
            end = end + self.lengths[0, s]
            start = jnp.where(self.qpos >= end, end, start)
        self.start = start

    def bias(self, slot):
        c = lax.axis_index("ctx")
        z = lax.rem(c, NZ)
        if isinstance(slot, int) and slot == OWN:
            base = c
        else:
            part = lax.rem(slot, NZ)
            near = c - z + part
            base = jnp.where(slot < NZ, jnp.where(part < z, near, near - 2 * NZ), near - NZ)
        pos = base * T + lax.broadcasted_iota(jnp.int32, (T, T), 0)
        visible = (pos >= self.start) & (pos <= self.qpos)
        return jnp.where(visible, 0.0, NEG).astype(jnp.float32)

    def forward(self, keys, values, bias, row, block, n):
        @pl.loop(0, KVH)
        def _(k):
            s = jnp.dot(keys(k), self.qt[k], preferred_element_type=jnp.float32)
            dp = jnp.dot(values(k), self.dot_[k], preferred_element_type=jnp.float32)
            self.dp[k, pl.ds(row, n), :] = dp
            for h in range(QPK):
                cols = slice(h * T, (h + 1) * T)
                x = s[:, cols] * (SCALE * LOG2E)
                if bias is not None:
                    x = x + bias
                old = self.m[k, :, cols]
                new = jnp.maximum(old, jnp.max(x, axis=0, keepdims=True))
                f = jnp.exp2(old - new)
                e = jnp.exp2(x - new)
                self.m[k, :, cols] = new
                self.mb[block, k, :, cols] = new
                self.l[k, :, cols] = self.l[k, :, cols] * f + jnp.sum(e, axis=0, keepdims=True)
                self.w[k, :, cols] = self.w[k, :, cols] * f + jnp.sum(e * dp[:, cols], axis=0, keepdims=True)
                self.e[k, pl.ds(row, n), cols] = e.astype(jnp.bfloat16)

    def slot_block(self, slot):
        bias = self.bias(slot)
        row = slot * T if isinstance(slot, int) else pl.multiple_of(slot * T, T)
        self.forward(
            lambda k: self.kv[slot, :, pl.ds(pl.multiple_of(k * D, D), D)],
            lambda k: self.kv[slot, :, pl.ds(pl.multiple_of(512 + k * D, D), D)],
            bias,
            row,
            slot,
            T,
        )

    def prompt_block(self):
        self.forward(
            lambda k: self.pg[0, :, pl.ds(pl.multiple_of(k * D, D), D)],
            lambda k: self.pg[1, :, pl.ds(pl.multiple_of(k * D, D), D)],
            None,
            PROMPT,
            17,
            PR,
        )

    def settle(self):
        self.l[...] = 1.0 / self.l[...]
        self.w[...] = self.w[...] * self.l[...]

    def grads(self, k, block, row, n):
        f = jnp.exp2(self.mb[block, k] - self.m[k]) * self.l[k]
        p = self.e[k, pl.ds(row, n), :].astype(jnp.float32) * f
        ds = (p * ((self.dp[k, pl.ds(row, n), :] - self.w[k]) * SCALE)).astype(jnp.bfloat16)
        return p, ds

    def add_dq(self, k, keys, ds):
        self.dq[k] += lax.dot_general(keys, ds, (((0,), (0,)), ((), ())), preferred_element_type=jnp.float32)

    def prompt_grads(self, part):
        @pl.loop(0, KVH)
        def _(k):
            cols = pl.ds(pl.multiple_of(k * D, D), D)
            p, ds = self.grads(k, 17, PROMPT, PR)
            part[0, :, cols] = jnp.dot(ds, self.qn[k], preferred_element_type=jnp.float32)
            part[1, :, cols] = jnp.dot(p.astype(jnp.bfloat16), self.don[k], preferred_element_type=jnp.float32)
            self.add_dq(k, self.pg[0, :, cols], ds)

    def slot_grads(self, slot):
        row = slot * T if isinstance(slot, int) else pl.multiple_of(slot * T, T)

        @pl.loop(0, KVH)
        def _(k):
            _, ds = self.grads(k, slot, row, T)
            self.add_dq(k, self.kv[slot, :, pl.ds(pl.multiple_of(k * D, D), D)], ds)

    def pair_grads(self, pair):
        row = pl.multiple_of(pair * 2 * T, 2 * T)

        @pl.loop(0, KVH)
        def _(k):
            _, d0 = self.grads(k, 2 * pair, row, T)
            _, d1 = self.grads(k, 2 * pair + 1, row + T, T)
            cols = pl.ds(pl.multiple_of(k * D, D), D)
            keys = self.kv[pl.ds(2 * pair, 2), :, cols].reshape(2 * T, D)
            self.add_dq(k, keys, jnp.concatenate([d0, d1], axis=0))

    def store(self, out):
        for k in range(KVH):
            for h in range(QPK):
                hd = k * QPK + h
                out[:, hd * D : (hd + 1) * D] = self.dq[k, :, h * T : (h + 1) * T].T.astype(jnp.bfloat16)


ATTEND_SCRATCH = [
    pltpu.VMEM((KVH, D, G), jnp.bfloat16),
    pltpu.VMEM((KVH, D, G), jnp.bfloat16),
    pltpu.VMEM((KVH, G, D), jnp.bfloat16),
    pltpu.VMEM((KVH, G, D), jnp.bfloat16),
    pltpu.VMEM((KVH, KEYS, G), jnp.bfloat16),
    pltpu.VMEM((KVH, KEYS, G), jnp.float32),
    pltpu.VMEM((KVH, 1, G), jnp.float32),
    pltpu.VMEM((KVH, 1, G), jnp.float32),
    pltpu.VMEM((KVH, 1, G), jnp.float32),
    pltpu.VMEM((18, KVH, 1, G), jnp.float32),
    pltpu.VMEM((KVH, D, G), jnp.float32),
]


def attend_kernel(q, do, kv, pg, lengths, dq, part, *scratch):
    a = Attend(q, do, kv, pg, lengths, scratch)
    a.prepare()
    a.slot_block(OWN)
    a.prompt_block()

    @pl.loop(0, 16)
    def _(slot):
        a.slot_block(slot)

    a.settle()
    a.prompt_grads(part)
    a.slot_grads(OWN)

    @pl.loop(0, 8)
    def _(pair):
        a.pair_grads(pair)

    a.store(dq)


class Reduce:
    def __init__(self, part, ko, vo, sc):
        self.part, self.ko, self.vo = part, ko, vo
        (self.s0, self.r0, self.acc, self.s1, self.r1, self.acc2, self.r2, self.s3, self.r3, self.ss, self.rs) = sc
        self.c, self.r, self.z, self.xy, self.role, self.mate = place()
        self.ylo = self.r // 2

    def peers(self):
        out = [(self.c, self.mate)]
        for s in range(1, NZ):
            out.append((self.xy * NZ + lax.rem(self.z + s, NZ), self.r))
        for s in range(1, 16):
            out.append(self.target(s)[:2])
        return out

    def target(self, s):
        me = self.xy * 2 + self.ylo
        other = lax.rem(me + s, 16)
        return (other // 2) * NZ + self.z, lax.rem(other, 2) * 2 + self.role, other

    def run(self):
        role, z, xy = self.role, self.z, self.xy
        self.s0[...] = self.part[1 - role].astype(jnp.bfloat16)
        first = remote(self.s0, self.r0, self.ss.at[0], self.rs.at[0], self.c, self.mate)
        first.start()
        first.wait_recv()
        for i in range(NXY):
            rows = slice(i * 64, (i + 1) * 64)
            self.acc[i] = (self.part[role, rows, :] + self.r0[rows, :].astype(jnp.float32)).reshape(NZ, 8, 512)
        for i in range(NZ):
            self.s1[i] = self.acc[:, i].reshape(64, 512).astype(jnp.bfloat16)
        copies = []
        for s in range(1, NZ):
            other = lax.rem(z + s, NZ)
            copies.append(
                remote(self.s1.at[other], self.r1.at[s], self.ss.at[s], self.rs.at[s], xy * NZ + other, self.r)
            )
        for copy in copies:
            copy.start()
        total = self.acc[:, z].reshape(64, 512)
        for s, copy in enumerate(copies, 1):
            copy.wait_recv()
            total = total + self.r1[s].astype(jnp.float32)
        self.acc2[...] = total.reshape(NXY, 8, 512)
        second = []
        for s in range(1, 16):
            ctx, resp, other = self.target(s)
            second.append(
                remote(self.acc2.at[other // 2], self.r2.at[s], self.ss.at[8 + s], self.rs.at[8 + s], ctx, resp)
            )
        for copy in second:
            copy.start()
        total = self.acc2[xy]
        for s, copy in enumerate(second, 1):
            copy.wait_recv()
            total = total + self.r2[s]
        self.s3[...] = total
        last = remote(self.s3, self.r3, self.ss.at[8], self.rs.at[8], self.c, self.mate)
        last.start()
        last.wait_recv()
        mine, other = self.s3[...], self.r3[...]
        self.ko[...] = jnp.where(role == 0, mine, other).astype(jnp.bfloat16)
        self.vo[...] = jnp.where(role == 0, other, mine).astype(jnp.bfloat16)
        for copy in [first] + copies + second + [last]:
            copy.wait_send()


REDUCE_SCRATCH = [
    pltpu.VMEM((512, 512), jnp.bfloat16),
    pltpu.VMEM((512, 512), jnp.bfloat16),
    pltpu.VMEM((NXY, NZ, 8, 512), jnp.float32),
    pltpu.VMEM((NZ, 64, 512), jnp.bfloat16),
    pltpu.VMEM((NZ, 64, 512), jnp.bfloat16),
    pltpu.VMEM((NXY, 8, 512), jnp.float32),
    pltpu.VMEM((16, 8, 512), jnp.float32),
    pltpu.VMEM((8, 512), jnp.float32),
    pltpu.VMEM((8, 512), jnp.float32),
    pltpu.SemaphoreType.DMA((24,)),
    pltpu.SemaphoreType.DMA((24,)),
]


def reduce_kernel(part, ko, vo, *scratch):
    r = Reduce(part, ko, vo, scratch)
    greet(r.peers())
    r.run()


VM = pl.BlockSpec(memory_space=pltpu.VMEM)
SM = pl.BlockSpec(memory_space=pltpu.SMEM)
MIB = 2**20


def body(queries, cotangent, sampled_keys, sampled_values, prompt_keys, prompt_values, lengths):
    kv, pg = pl.pallas_call(
        gather_kernel,
        out_shape=(
            jax.ShapeDtypeStruct((17, T, 1024), jnp.bfloat16),
            jax.ShapeDtypeStruct((2, PR, 512), jnp.bfloat16),
        ),
        in_specs=[VM] * 4,
        out_specs=(VM, VM),
        scratch_shapes=[
            pltpu.VMEM((NZ, 8, 512), jnp.float32),
            pltpu.SemaphoreType.DMA((20,)),
            pltpu.SemaphoreType.DMA((17,)),
            pltpu.SemaphoreType.DMA((16,)),
            pltpu.SemaphoreType.DMA((16,)),
        ],
        compiler_params=pltpu.CompilerParams(
            collective_id=0, has_side_effects=True, vmem_limit_bytes=32 * MIB
        ),
        name="gather",
    )(sampled_keys[0], sampled_values[0], prompt_keys, prompt_values)
    dq, part = pl.pallas_call(
        attend_kernel,
        out_shape=(
            jax.ShapeDtypeStruct((T, HQ * D), jnp.bfloat16),
            jax.ShapeDtypeStruct((2, PR, 512), jnp.float32),
        ),
        in_specs=[VM] * 4 + [SM],
        out_specs=(VM, VM),
        scratch_shapes=ATTEND_SCRATCH,
        compiler_params=pltpu.CompilerParams(vmem_limit_bytes=60 * MIB),
        name="attend",
    )(queries[0], cotangent[0], kv, pg, lengths)
    ko, vo = pl.pallas_call(
        reduce_kernel,
        out_shape=(jax.ShapeDtypeStruct((8, 512), jnp.bfloat16),) * 2,
        in_specs=[VM],
        out_specs=(VM, VM),
        scratch_shapes=REDUCE_SCRATCH,
        compiler_params=pltpu.CompilerParams(
            collective_id=1, has_side_effects=True, vmem_limit_bytes=32 * MIB
        ),
        name="reduce",
    )(part)
    return dq[None], ko, vo


def solution(mesh):
    rows = P("resp", "ctx", None)
    in_specs = (rows, rows, rows, rows, P("ctx", None), P("ctx", None), P("resp", None))
    out_specs = (rows, P("ctx", None), P("ctx", None))
    return jax.shard_map(body, mesh=mesh, in_specs=in_specs, out_specs=out_specs, check_vma=False)
```

time: 1290 us -> 158 us (0.12)
  waiting for transfers between devices: 694 us -> 0 us
  blocking collectives: 365 us -> 0 us
  Pallas kernels: 0 us -> 147 us
  starting transfers between devices: 116 us -> 0 us
  matrix products: 67.6 us -> 0 us
  between operations: 16 us -> 0.67 us
  other arithmetic: 13.9 us -> 0 us
    reduce_scatter x2 -> x0, waiting for transfers between devices: 694 us -> none  [the longest x1 359 us: body(): lax.psum_scatter(flattened_values, 'ctx', scatter_dimension=0, tiled=True)]
    all_gather x2 -> x0, blocking collectives: 301 us -> none  [the longest x1 151 us: body(): lax.all_gather(shared_prompt_values, 'ctx', axis=0, tiled=True)]
    pallas_call x0 -> x3, Pallas kernels: none -> 147 us  [the longest x1 76.9 us: body(): pl.pallas_call(gather_kernel, out_shape=(jax.ShapeDtypeStruct((17, T, 102...]
    ppermute x32 -> x0, starting transfers between devices: 116 us -> none  [passed_along(): return lax.ppermute(value, axis, pairs)]
    dot_general x56 -> x0, matrix products: 67.6 us -> none  [the longest x17 33.3 us: body(): jnp.einsum('rkqj,jkd->rkqd', response_logit_low, response_heads_of_keys,...]
    psum x1 -> x0, blocking collectives: 63.9 us -> none  [body(): key_whole, value_whole = lax.psum((key_part, value_part), 'resp')]
  transfers between devices with their start and end apart: 34 -> 0, of which waited for: 3 -> 0; matrix products, arithmetic and copies ran while one was open for 5% -> 0% of each run, Pallas kernels for 0% -> 0%
where the time goes in v1:
time: 158 us; the launch traced here: 157 us
  Pallas kernels  147 us (93%)
  local copies, waits for them, and re-layouts  8.97 us (6%)
    pallas_call x1, Pallas kernels, body(): pl.pallas_call(gather_kernel, out_shape=(jax.ShapeDtypeStruct((17, T, 102...  76.9 us
    pallas_call x1, Pallas kernels, body(): pl.pallas_call(attend_kernel, out_shape=(jax.ShapeDtypeStruct((T, HQ * D)...  41.8 us
    pallas_call x1, Pallas kernels, body(): pl.pallas_call(reduce_kernel, out_shape=(jax.ShapeDtypeStruct((8, 512), j...  28.6 us
    unnamed x16, local copies, waits for them, and re-layouts  8.97 us

profile of v1, /device:TPU:1, one launch (start us, length us, event | category | flops | bytes accessed | tf_op | source)
XLA Modules:
  0.0 156.9 jit_solution(15025995986576314331)
XLA Ops:
  0.6 0.0 copy-start.3
  0.6 0.9 copy-done.3
  1.5 0.0 copy-start.4
  1.5 0.9 copy-done.4
  2.4 0.0 copy-start.5
  2.4 0.7 copy-done.5
  3.1 0.0 copy-start.6
  3.1 0.7 copy-done.6
  3.8 76.9 %gather.1 = (bf16[17,128,1024]{2,1,0:T(8,128)(2,1)S(1)}, bf16[2,512,512]{2,1,0:T(8,128)(2,1)S(1)}) custom-call(bf16[128,512]{1,0:T(8,128)(2,1)S(1)} %bitcast.5, bf16[128,512]{1,0:T(8,128)(2,1)S(1)} %bitcast.6, bf16[8,512]{1,0:T(8,128)(2,1)S(1)} %copy-done.5, bf16[8,512]{1,0:T(8,128)(2,1)S(1)} %copy-done.6), custom_call_target="tpu_custom_call" | custom-call | tf_op jit(solution)/shard_map/gather/pallas_call | solution.py:478
  80.7 0.0 copy-start
  80.8 2.0 %copy-done = bf16[17,128,1024]{2,1,0:T(8,128)(2,1)} copy-done((bf16[17,128,1024]{2,1,0:T(8,128)(2,1)}, bf16[17,128,1024]{2,1,0:T(8,128)(2,1)S(1)}, u32[]{:S(2)}) %copy-start) | copy-done | bytes 4456472
  82.8 0.0 copy-start.2
  82.8 1.0 copy-done.2
  83.7 41.8 %attend.1 = (bf16[128,2560]{1,0:T(8,128)(2,1)}, f32[2,512,512]{2,1,0:T(8,128)}) custom-call(bf16[128,2560]{1,0:T(8,128)(2,1)} %bitcast.7, bf16[128,2560]{1,0:T(8,128)(2,1)} %bitcast.8, bf16[17,128,1024]{2,1,0:T(8,128)(2,1)} %copy-done, bf16[2,512,512]{2,1,0:T(8,128)(2,1)} %copy-done.2, s32[1,8]{1,0:T(1,128)} %lengths.1), custom_call_target="tpu_custom_call" | custom-call | tf_op jit(solution)/shard_map/attend/pallas_call | solution.py:498
  125.5 0.0 copy-start.1
  125.5 1.6 %copy-done.1 = f32[2,512,512]{2,1,0:T(8,128)S(1)} copy-done((f32[2,512,512]{2,1,0:T(8,128)S(1)}, f32[2,512,512]{2,1,0:T(8,128)}, u32[]{:S(2)}) %copy-start.1) | copy-done | bytes 2097176
  127.1 28.6 %reduce.1 = (bf16[8,512]{1,0:T(8,128)(2,1)S(1)}, bf16[8,512]{1,0:T(8,128)(2,1)S(1)}) custom-call(f32[2,512,512]{2,1,0:T(8,128)S(1)} %copy-done.1), custom_call_target="tpu_custom_call" | custom-call | tf_op jit(solution)/shard_map/reduce/pallas_call | solution.py:510
  155.7 0.6 copy.12
  156.3 0.6 copy.13
Async XLA Ops:
  0.6 0.9 copy-start.3
  1.5 0.9 copy-start.4
  2.4 0.7 copy-start.5
  3.1 0.7 copy-start.6
  80.7 2.0 %copy-start = (bf16[17,128,1024]{2,1,0:T(8,128)(2,1)}, bf16[17,128,1024]{2,1,0:T(8,128)(2,1)S(1)}, u32[]{:S(2)}) copy-start(bf16[17,128,1024]{2,1,0:T(8,128)(2,1)S(1)} %get-tuple-element.9.kv) | copy-start | bytes 13369348
  82.8 1.0 copy-start.2
  125.5 1.6 %copy-start.1 = (f32[2,512,512]{2,1,0:T(8,128)S(1)}, f32[2,512,512]{2,1,0:T(8,128)}, u32[]{:S(2)}) copy-start(f32[2,512,512]{2,1,0:T(8,128)} %get-tuple-element.12.part) | copy-start | bytes 6291460

commit v2 on v1

--- a/solution.py
+++ b/solution.py
@@ -1,5 +1,3 @@
-import functools
-
 import jax
 import jax.numpy as jnp
 from jax import lax
@@ -85,29 +83,29 @@
             (z < NZ - 1, self.piece(OWN, z, 18, self.c + 1)),
         ]
 
-    def step(self, s):
-        z, c = self.z, self.c
+    def candidate(self, s, i):
+        z = self.z
+        low, high = lax.rem(z - s + NZ, NZ), lax.rem(z + s, NZ)
+        if i == 0:
+            return z >= s, low, True, z < NZ - 1
+        if i == 1:
+            return (s > 0) & (z + s < NZ), high, False, z > 0
+        if i == 2:
+            return s <= UP, NZ + low, True, s < UP
+        return (s > 0) & (s <= DOWN), NZ + high, False, s < DOWN
+
+    def onward(self, slot, up):
+        to = lax.rem(self.z + (1 if up else NZ - 1), NZ)
+        return self.piece(slot, slot, slot, self.xy * NZ + to)
+
+    def first_sends(self):
+        z = self.z
         up = self.xy * NZ + lax.rem(z + 1, NZ)
-        down = self.xy * NZ + lax.rem(z + NZ - 1, NZ)
-        if s == 0:
-            return [
-                (None, z, [(z > 0, self.piece(z, z, z, down))]),
-                (
-                    None,
-                    8 + z,
-                    [(None, self.piece(8 + z, 8 + z, 19, up)), (None, self.piece(8 + z, 8 + z, 8 + z, down))],
-                ),
-            ]
-        low, high = lax.rem(z - s + NZ, NZ), lax.rem(z + s, NZ)
-        out = [
-            (z >= s, low, [(z < NZ - 1, self.piece(low, low, low, up))]),
-            (z + s < NZ, high, [(z > 0, self.piece(high, high, high, down))]),
+        return [
+            (z > 0, self.onward(z, False)),
+            (None, self.piece(NZ + z, NZ + z, 19, up)),
+            (None, self.onward(NZ + z, False)),
         ]
-        if s <= UP:
-            out.append((None, 8 + low, [(None, self.piece(8 + low, 8 + low, 8 + low, up))] if s < UP else []))
-        if s <= DOWN:
-            out.append((None, 8 + high, [(None, self.piece(8 + high, 8 + high, 8 + high, down))] if s < DOWN else []))
-        return out
 
     @staticmethod
     def when(condition, do):
@@ -120,27 +118,30 @@
         for condition, copy in self.own_sends():
             self.when(condition, copy.start)
 
+    def take_first(self):
+        self.arrived(self.z)
+        self.arrived(NZ + self.z)
+        for condition, copy in self.first_sends():
+            self.when(condition, copy.start)
+
     def take_step(self, s):
-        for condition, slot, sends in self.step(s):
-
-            def take(slot=slot, sends=sends):
+        for i in range(4):
+            condition, slot, up, more = self.candidate(s, i)
+
+            @pl.when(condition)
+            def _(slot=slot, up=up, more=more):
                 self.arrived(slot)
-                for inner, copy in sends:
-                    self.when(inner, copy.start)
-
-            self.when(condition, take)
+                pl.when(more)(self.onward(slot, up).start)
 
     def finish(self):
-        for condition, copy in self.own_sends():
+        for condition, copy in self.own_sends() + self.first_sends():
             self.when(condition, copy.wait_send)
-        for s in range(NZ):
-            for condition, slot, sends in self.step(s):
-
-                def done(sends=sends):
-                    for inner, copy in sends:
-                        self.when(inner, copy.wait_send)
-
-                self.when(condition, done)
+
+        @pl.loop(1, NZ)
+        def _(s):
+            for i in range(4):
+                condition, slot, up, more = self.candidate(s, i)
+                pl.when(condition & more)(self.onward(slot, up).wait_send)
 
     def prompt_z(self, pk, pv):
         z = self.z
@@ -193,30 +194,17 @@
     def prompt_done(self):
         other = self.pg.at[1 - self.role]
         remote(other, other, self.ps.at[0], self.pr.at[0], self.c, self.mate).wait_recv()
+
+    def prompt_sent(self):
         for copy in self.zcopies + self.xycopies + [self.corecopy]:
             copy.wait_send()
-
-
-def gather_kernel(k, v, pk, pv, kv, pg, za, ks, kr, ps, pr):
-    g = Gather(kv, pg, za, ks, kr, ps, pr)
-    kv[OWN, :, :512] = k[...]
-    kv[OWN, :, 512:] = v[...]
-    greet(g.peers())
-    g.prompt_z(pk, pv)
-    g.start_own()
-    g.prompt_xy()
-    g.take_step(0)
-    g.prompt_core()
-    for s in range(1, NZ):
-        g.take_step(s)
-    g.prompt_done()
-    g.finish()
 
 
 class Attend:
     def __init__(self, q, do, kv, pg, lengths, sc):
         self.q, self.do, self.kv, self.pg, self.lengths = q, do, kv, pg, lengths
-        (self.qt, self.dot_, self.qn, self.don, self.e, self.dp, self.m, self.l, self.w, self.mb, self.dq) = sc
+        (self.qt, self.dot_, self.qn, self.don, self.e, self.ep, self.dp) = sc[:7]
+        (self.m, self.l, self.w, self.mb, self.dq) = sc[7:]
 
     def prepare(self):
         for k in range(KVH):
@@ -273,7 +261,10 @@
                 self.mb[block, k, :, cols] = new
                 self.l[k, :, cols] = self.l[k, :, cols] * f + jnp.sum(e, axis=0, keepdims=True)
                 self.w[k, :, cols] = self.w[k, :, cols] * f + jnp.sum(e * dp[:, cols], axis=0, keepdims=True)
-                self.e[k, pl.ds(row, n), cols] = e.astype(jnp.bfloat16)
+                if bias is None:
+                    self.ep[k, pl.ds(row - PROMPT, n), cols] = e
+                else:
+                    self.e[k, pl.ds(row, n), cols] = e.astype(jnp.bfloat16)
 
     def slot_block(self, slot):
         bias = self.bias(slot)
@@ -287,25 +278,29 @@
             T,
         )
 
-    def prompt_block(self):
+    def prompt_block(self, i):
+        rows = pl.ds(pl.multiple_of(i * T, T), T)
         self.forward(
-            lambda k: self.pg[0, :, pl.ds(pl.multiple_of(k * D, D), D)],
-            lambda k: self.pg[1, :, pl.ds(pl.multiple_of(k * D, D), D)],
+            lambda k: self.pg[0, rows, pl.ds(pl.multiple_of(k * D, D), D)],
+            lambda k: self.pg[1, rows, pl.ds(pl.multiple_of(k * D, D), D)],
             None,
-            PROMPT,
-            17,
-            PR,
+            pl.multiple_of(PROMPT + i * T, T),
+            17 + i,
+            T,
         )
 
     def settle(self):
         self.l[...] = 1.0 / self.l[...]
         self.w[...] = self.w[...] * self.l[...]
 
-    def grads(self, k, block, row, n):
+    def grads(self, k, block, row, e):
         f = jnp.exp2(self.mb[block, k] - self.m[k]) * self.l[k]
-        p = self.e[k, pl.ds(row, n), :].astype(jnp.float32) * f
-        ds = (p * ((self.dp[k, pl.ds(row, n), :] - self.w[k]) * SCALE)).astype(jnp.bfloat16)
+        p = e * f
+        ds = (p * ((self.dp[k, pl.ds(row, T), :] - self.w[k]) * SCALE)).astype(jnp.bfloat16)
         return p, ds
+
+    def slot_e(self, k, row):
+        return self.e[k, pl.ds(row, T), :].astype(jnp.float32)
 
     def add_dq(self, k, keys, ds):
         self.dq[k] += lax.dot_general(keys, ds, (((0,), (0,)), ((), ())), preferred_element_type=jnp.float32)
@@ -314,9 +309,14 @@
         @pl.loop(0, KVH)
         def _(k):
             cols = pl.ds(pl.multiple_of(k * D, D), D)
-            p, ds = self.grads(k, 17, PROMPT, PR)
-            part[0, :, cols] = jnp.dot(ds, self.qn[k], preferred_element_type=jnp.float32)
-            part[1, :, cols] = jnp.dot(p.astype(jnp.bfloat16), self.don[k], preferred_element_type=jnp.float32)
+            blocks = []
+            for i in range(4):
+                rows = slice(i * T, (i + 1) * T)
+                p, ds = self.grads(k, 17 + i, PROMPT + i * T, self.ep[k, rows, :])
+                blocks.append(ds)
+                part[0, rows, cols] = jnp.dot(ds, self.qn[k], preferred_element_type=jnp.float32)
+                part[1, rows, cols] = jnp.dot(p.astype(jnp.bfloat16), self.don[k], preferred_element_type=jnp.float32)
+            ds = jnp.concatenate(blocks, axis=0)
             self.add_dq(k, self.pg[0, :, cols], ds)
 
     def slot_grads(self, slot):
@@ -324,7 +324,7 @@
 
         @pl.loop(0, KVH)
         def _(k):
-            _, ds = self.grads(k, slot, row, T)
+            _, ds = self.grads(k, slot, row, self.slot_e(k, row))
             self.add_dq(k, self.kv[slot, :, pl.ds(pl.multiple_of(k * D, D), D)], ds)
 
     def pair_grads(self, pair):
@@ -332,8 +332,8 @@
 
         @pl.loop(0, KVH)
         def _(k):
-            _, d0 = self.grads(k, 2 * pair, row, T)
-            _, d1 = self.grads(k, 2 * pair + 1, row + T, T)
+            _, d0 = self.grads(k, 2 * pair, row, self.slot_e(k, row))
+            _, d1 = self.grads(k, 2 * pair + 1, row + T, self.slot_e(k, row + T))
             cols = pl.ds(pl.multiple_of(k * D, D), D)
             keys = self.kv[pl.ds(2 * pair, 2), :, cols].reshape(2 * T, D)
             self.add_dq(k, keys, jnp.concatenate([d0, d1], axis=0))
@@ -350,35 +350,15 @@
     pltpu.VMEM((KVH, D, G), jnp.bfloat16),
     pltpu.VMEM((KVH, G, D), jnp.bfloat16),
     pltpu.VMEM((KVH, G, D), jnp.bfloat16),
-    pltpu.VMEM((KVH, KEYS, G), jnp.bfloat16),
+    pltpu.VMEM((KVH, 17 * T, G), jnp.bfloat16),
+    pltpu.VMEM((KVH, PR, G), jnp.float32),
     pltpu.VMEM((KVH, KEYS, G), jnp.float32),
     pltpu.VMEM((KVH, 1, G), jnp.float32),
     pltpu.VMEM((KVH, 1, G), jnp.float32),
     pltpu.VMEM((KVH, 1, G), jnp.float32),
-    pltpu.VMEM((18, KVH, 1, G), jnp.float32),
+    pltpu.VMEM((21, KVH, 1, G), jnp.float32),
     pltpu.VMEM((KVH, D, G), jnp.float32),
 ]
-
-
-def attend_kernel(q, do, kv, pg, lengths, dq, part, *scratch):
-    a = Attend(q, do, kv, pg, lengths, scratch)
-    a.prepare()
-    a.slot_block(OWN)
-    a.prompt_block()
-
-    @pl.loop(0, 16)
-    def _(slot):
-        a.slot_block(slot)
-
-    a.settle()
-    a.prompt_grads(part)
-    a.slot_grads(OWN)
-
-    @pl.loop(0, 8)
-    def _(pair):
-        a.pair_grads(pair)
-
-    a.store(dq)
 
 
 class Reduce:
@@ -401,50 +381,58 @@
         other = lax.rem(me + s, 16)
         return (other // 2) * NZ + self.z, lax.rem(other, 2) * 2 + self.role, other
 
-    def run(self):
-        role, z, xy = self.role, self.z, self.xy
-        self.s0[...] = self.part[1 - role].astype(jnp.bfloat16)
-        first = remote(self.s0, self.r0, self.ss.at[0], self.rs.at[0], self.c, self.mate)
-        first.start()
-        first.wait_recv()
+    def core_start(self):
+        self.s0[...] = self.part[1 - self.role].astype(jnp.bfloat16)
+        self.first = remote(self.s0, self.r0, self.ss.at[0], self.rs.at[0], self.c, self.mate)
+        self.first.start()
+
+    def z_start(self):
+        z = self.z
+        self.first.wait_recv()
         for i in range(NXY):
             rows = slice(i * 64, (i + 1) * 64)
-            self.acc[i] = (self.part[role, rows, :] + self.r0[rows, :].astype(jnp.float32)).reshape(NZ, 8, 512)
+            self.acc[i] = (self.part[self.role, rows, :] + self.r0[rows, :].astype(jnp.float32)).reshape(NZ, 8, 512)
         for i in range(NZ):
             self.s1[i] = self.acc[:, i].reshape(64, 512).astype(jnp.bfloat16)
-        copies = []
+        self.copies = []
         for s in range(1, NZ):
             other = lax.rem(z + s, NZ)
-            copies.append(
-                remote(self.s1.at[other], self.r1.at[s], self.ss.at[s], self.rs.at[s], xy * NZ + other, self.r)
+            self.copies.append(
+                remote(self.s1.at[other], self.r1.at[s], self.ss.at[s], self.rs.at[s], self.xy * NZ + other, self.r)
             )
-        for copy in copies:
+        for copy in self.copies:
             copy.start()
-        total = self.acc[:, z].reshape(64, 512)
-        for s, copy in enumerate(copies, 1):
+
+    def ring_start(self):
+        total = self.acc[:, self.z].reshape(64, 512)
+        for s, copy in enumerate(self.copies, 1):
             copy.wait_recv()
             total = total + self.r1[s].astype(jnp.float32)
         self.acc2[...] = total.reshape(NXY, 8, 512)
-        second = []
+        self.second = []
         for s in range(1, 16):
             ctx, resp, other = self.target(s)
-            second.append(
+            self.second.append(
                 remote(self.acc2.at[other // 2], self.r2.at[s], self.ss.at[8 + s], self.rs.at[8 + s], ctx, resp)
             )
-        for copy in second:
+        for copy in self.second:
             copy.start()
-        total = self.acc2[xy]
-        for s, copy in enumerate(second, 1):
+
+    def mate_start(self):
+        total = self.acc2[self.xy]
+        for s, copy in enumerate(self.second, 1):
             copy.wait_recv()
             total = total + self.r2[s]
         self.s3[...] = total
-        last = remote(self.s3, self.r3, self.ss.at[8], self.rs.at[8], self.c, self.mate)
-        last.start()
-        last.wait_recv()
+        self.last = remote(self.s3, self.r3, self.ss.at[8], self.rs.at[8], self.c, self.mate)
+        self.last.start()
+
+    def finish(self):
+        self.last.wait_recv()
         mine, other = self.s3[...], self.r3[...]
-        self.ko[...] = jnp.where(role == 0, mine, other).astype(jnp.bfloat16)
-        self.vo[...] = jnp.where(role == 0, other, mine).astype(jnp.bfloat16)
-        for copy in [first] + copies + second + [last]:
+        self.ko[...] = jnp.where(self.role == 0, mine, other).astype(jnp.bfloat16)
+        self.vo[...] = jnp.where(self.role == 0, other, mine).astype(jnp.bfloat16)
+        for copy in [self.first] + self.copies + self.second + [self.last]:
             copy.wait_send()
 
 
@@ -463,61 +451,112 @@
 ]
 
 
-def reduce_kernel(part, ko, vo, *scratch):
-    r = Reduce(part, ko, vo, scratch)
+GATHER_SCRATCH = [
+    pltpu.VMEM((17, T, 1024), jnp.bfloat16),
+    pltpu.VMEM((2, PR, 512), jnp.bfloat16),
+    pltpu.VMEM((NZ, 8, 512), jnp.float32),
+    pltpu.SemaphoreType.DMA((20,)),
+    pltpu.SemaphoreType.DMA((16,)),
+    pltpu.SemaphoreType.DMA((16,)),
+    pltpu.SemaphoreType.DMA((16,)),
+]
+OWN_SCRATCH = [
+    pltpu.VMEM((T, HQ * D), jnp.bfloat16),
+    pltpu.VMEM((T, HQ * D), jnp.bfloat16),
+    pltpu.VMEM((2, PR, 512), jnp.float32),
+    pltpu.SemaphoreType.DMA((4,)),
+]
+
+
+def kernel(q_in, do_in, k_in, v_in, pk, pv, lengths, dq, ko, vo, *scratch):
+    ng, no, na = len(GATHER_SCRATCH), len(OWN_SCRATCH), len(ATTEND_SCRATCH)
+    gather_refs, own_refs = scratch[:ng], scratch[ng : ng + no]
+    q, do, part, sems = own_refs
+    g = Gather(*gather_refs)
+    r = Reduce(part, ko, vo, scratch[ng + no + na :])
+    a = Attend(q, do, g.kv, g.pg, lengths, scratch[ng + no : ng + no + na])
+    loads = [
+        pltpu.make_async_copy(k_in, g.kv.at[OWN, :, pl.ds(0, 512)], sems.at[0]),
+        pltpu.make_async_copy(v_in, g.kv.at[OWN, :, pl.ds(512, 512)], sems.at[1]),
+        pltpu.make_async_copy(q_in, q, sems.at[2]),
+        pltpu.make_async_copy(do_in, do, sems.at[3]),
+    ]
+    for copy in loads:
+        copy.start()
     greet(r.peers())
-    r.run()
+    g.prompt_z(pk, pv)
+    loads[0].wait()
+    loads[1].wait()
+    g.start_own()
+    loads[2].wait()
+    loads[3].wait()
+    a.prepare()
+    g.prompt_xy()
+    g.take_first()
+    a.slot_block(OWN)
+    g.prompt_core()
+
+    @pl.loop(1, NZ + 1)
+    def _(s):
+        pl.when(s < NZ)(lambda: g.take_step(s))
+
+        @pl.loop(0, 4)
+        def _(i):
+            choices = [g.candidate(s - 1, j) for j in range(4)]
+            present, slot = choices[0][0], choices[0][1]
+            for j in range(1, 4):
+                present = jnp.where(i == j, choices[j][0].astype(jnp.int32), present.astype(jnp.int32))
+                slot = jnp.where(i == j, choices[j][1], slot)
+            pl.when(present > 0)(lambda: a.slot_block(slot))
+
+        pl.when(s == 2)(g.prompt_done)
+        pl.when((s > 2) & (s < 7))(lambda: a.prompt_block(s - 3))
+
+    a.settle()
+    a.prompt_grads(part)
+    r.core_start()
+    a.slot_grads(OWN)
+    r.z_start()
+
+    @pl.loop(0, 5)
+    def _(pair):
+        a.pair_grads(pair)
+
+    r.ring_start()
+
+    @pl.loop(5, 8)
+    def _(pair):
+        a.pair_grads(pair)
+
+    r.mate_start()
+    a.store(dq)
+    r.finish()
+    g.prompt_sent()
+    g.finish()
 
 
 VM = pl.BlockSpec(memory_space=pltpu.VMEM)
 SM = pl.BlockSpec(memory_space=pltpu.SMEM)
+ANY = pl.BlockSpec(memory_space=pl.ANY)
 MIB = 2**20
 
 
 def body(queries, cotangent, sampled_keys, sampled_values, prompt_keys, prompt_values, lengths):
-    kv, pg = pl.pallas_call(
-        gather_kernel,
-        out_shape=(
-            jax.ShapeDtypeStruct((17, T, 1024), jnp.bfloat16),
-            jax.ShapeDtypeStruct((2, PR, 512), jnp.bfloat16),
-        ),
-        in_specs=[VM] * 4,
-        out_specs=(VM, VM),
-        scratch_shapes=[
-            pltpu.VMEM((NZ, 8, 512), jnp.float32),
-            pltpu.SemaphoreType.DMA((20,)),
-            pltpu.SemaphoreType.DMA((17,)),
-            pltpu.SemaphoreType.DMA((16,)),
-            pltpu.SemaphoreType.DMA((16,)),
-        ],
-        compiler_params=pltpu.CompilerParams(
-            collective_id=0, has_side_effects=True, vmem_limit_bytes=32 * MIB
-        ),
-        name="gather",
-    )(sampled_keys[0], sampled_values[0], prompt_keys, prompt_values)
-    dq, part = pl.pallas_call(
-        attend_kernel,
+    dq, ko, vo = pl.pallas_call(
+        kernel,
         out_shape=(
             jax.ShapeDtypeStruct((T, HQ * D), jnp.bfloat16),
-            jax.ShapeDtypeStruct((2, PR, 512), jnp.float32),
+            jax.ShapeDtypeStruct((8, 512), jnp.bfloat16),
+            jax.ShapeDtypeStruct((8, 512), jnp.bfloat16),
         ),
-        in_specs=[VM] * 4 + [SM],
-        out_specs=(VM, VM),
-        scratch_shapes=ATTEND_SCRATCH,
-        compiler_params=pltpu.CompilerParams(vmem_limit_bytes=60 * MIB),
-        name="attend",
-    )(queries[0], cotangent[0], kv, pg, lengths)
-    ko, vo = pl.pallas_call(
-        reduce_kernel,
-        out_shape=(jax.ShapeDtypeStruct((8, 512), jnp.bfloat16),) * 2,
-        in_specs=[VM],
-        out_specs=(VM, VM),
-        scratch_shapes=REDUCE_SCRATCH,
+        in_specs=[ANY] * 4 + [VM] * 2 + [SM],
+        out_specs=(VM, VM, VM),
+        scratch_shapes=GATHER_SCRATCH + OWN_SCRATCH + ATTEND_SCRATCH + REDUCE_SCRATCH,
         compiler_params=pltpu.CompilerParams(
-            collective_id=1, has_side_effects=True, vmem_limit_bytes=32 * MIB
+            collective_id=0, has_side_effects=True, vmem_limit_bytes=62 * MIB
         ),
-        name="reduce",
-    )(part)
+        name="shared_prompt_backward",
+    )(queries[0], cotangent[0], sampled_keys[0], sampled_values[0], prompt_keys, prompt_values, lengths)
     return dq[None], ko, vo
 
 

time: 158 us -> 117 us (0.74)
  the two profiles are of different devices: /device:TPU:1 before, /device:TPU:153 now
where the time goes in v2:
time: 117 us
  Pallas kernels  113 us (97%)
  local copies, waits for them, and re-layouts  3.27 us (3%)
    pallas_call x1, Pallas kernels, body(): pl.pallas_call(kernel, out_shape=(jax.ShapeDtypeStruct((T, HQ * D), jnp.b...  113 us
    unnamed x7, local copies, waits for them, and re-layouts  3.27 us

profile of v2, /device:TPU:153, one launch (start us, length us, event | category | flops | bytes accessed | tf_op | source)
XLA Modules:
  0.0 117.0 jit_solution(10824789251780593496)
XLA Ops:
  0.6 113.0 %shared_prompt_backward.1 = (bf16[128,2560]{1,0:T(8,128)(2,1)}, bf16[8,512]{1,0:T(8,128)(2,1)}, bf16[8,512]{1,0:T(8,128)(2,1)}) custom-call(bf16[128,2560]{1,0:T(8,128)(2,1)} %bitcast.5, bf16[128,2560]{1,0:T(8,128)(2,1)} %bitcast.6, bf16[128,512]{1,0:T(8,128)(2,1)} %bitcast.8, bf16[128,512]{1,0:T(8,128)(2,1)} %bitcast.9, bf16[8,512]{1,0:T(8,128)(2,1)} %pk.1, ...), custom_call_target="tpu_custom_call" | custom-call | tf_op jit(solution)/shard_map/shared_prompt_backward/pallas_call | solution.py:545
  113.7 0.0 copy-start.1
  113.7 2.0 %copy.13 = bf16[1,128,2560]{2,1,0:T(8,128)(2,1)} copy(bf16[1,128,2560]{2,1,0:T(8,128)(2,1)} %bitcast.7) | data formatting | bytes 1310720
  115.6 0.0 copy-done.1
  115.7 0.0 copy-start
  115.7 0.6 copy.14
  116.3 0.1 copy-done
  116.4 0.6 copy.15
Async XLA Ops:
  113.7 2.0 %copy-start.1 = (bf16[8,512]{1,0:T(8,128)(2,1)S(1)}, bf16[8,512]{1,0:T(8,128)(2,1)}, u32[]{:S(2)}) copy-start(bf16[8,512]{1,0:T(8,128)(2,1)} %get-tuple-element.13) | copy-start | bytes 24580
  115.7 0.7 copy-start

commit v3 on v2

--- a/solution.py
+++ b/solution.py
@@ -14,8 +14,13 @@
 G = QPK * T
 NZ = 8
 NXY = 8
-UP = 4
-DOWN = NZ - 1 - UP
+ROUNDS = 6
+NONE = 31
+FROM_BELOW = (416751103, 216251648, 477602817, 1056210978, 508888131, 1050708068, 1041304709, 35754150)
+FROM_ABOVE = (137734463, 181808479, 207008127, 273102239, 241187263, 510853599, 317956127, 1052058880)
+FROM_BEFORE = (174130184, 1044482089, 1043472458, 241346667, 1048882316, 412363949, 380022990, 1053210863)
+TO_ABOVE = (216251664, 477602832, 1056210992, 508888144, 1050708080, 1041304720, 35754160, 416751103)
+TO_BELOW = (1052058896, 137734463, 181808479, 207008127, 273102239, 241187263, 510853599, 317956127)
 SCALE = D ** (-0.5)
 LOG2E = 1.4426950408889634
 NEG = -1e30
@@ -73,40 +78,6 @@
     def arrived(self, slot):
         self.piece(slot, slot, slot, self.c).wait_recv()
 
-    def own_sends(self):
-        z = self.z
-        after = lax.rem(self.c + NZ, NZ * NXY)
-        second = lax.rem(self.c + 2 * NZ, NZ * NXY)
-        return [
-            (None, self.piece(OWN, z, 17, second)),
-            (None, self.piece(OWN, 8 + z, 16, after)),
-            (z < NZ - 1, self.piece(OWN, z, 18, self.c + 1)),
-        ]
-
-    def candidate(self, s, i):
-        z = self.z
-        low, high = lax.rem(z - s + NZ, NZ), lax.rem(z + s, NZ)
-        if i == 0:
-            return z >= s, low, True, z < NZ - 1
-        if i == 1:
-            return (s > 0) & (z + s < NZ), high, False, z > 0
-        if i == 2:
-            return s <= UP, NZ + low, True, s < UP
-        return (s > 0) & (s <= DOWN), NZ + high, False, s < DOWN
-
-    def onward(self, slot, up):
-        to = lax.rem(self.z + (1 if up else NZ - 1), NZ)
-        return self.piece(slot, slot, slot, self.xy * NZ + to)
-
-    def first_sends(self):
-        z = self.z
-        up = self.xy * NZ + lax.rem(z + 1, NZ)
-        return [
-            (z > 0, self.onward(z, False)),
-            (None, self.piece(NZ + z, NZ + z, 19, up)),
-            (None, self.onward(NZ + z, False)),
-        ]
-
     @staticmethod
     def when(condition, do):
         if condition is None:
@@ -114,34 +85,53 @@
         else:
             pl.when(condition)(do)
 
-    def start_own(self):
-        for condition, copy in self.own_sends():
-            self.when(condition, copy.start)
-
-    def take_first(self):
-        self.arrived(self.z)
-        self.arrived(NZ + self.z)
-        for condition, copy in self.first_sends():
-            self.when(condition, copy.start)
-
-    def take_step(self, s):
-        for i in range(4):
-            condition, slot, up, more = self.candidate(s, i)
-
-            @pl.when(condition)
-            def _(slot=slot, up=up, more=more):
-                self.arrived(slot)
-                pl.when(more)(self.onward(slot, up).start)
-
-    def finish(self):
-        for condition, copy in self.own_sends() + self.first_sends():
-            self.when(condition, copy.wait_send)
-
-        @pl.loop(1, NZ)
-        def _(s):
-            for i in range(4):
-                condition, slot, up, more = self.candidate(s, i)
-                pl.when(condition & more)(self.onward(slot, up).wait_send)
+    def tables(self):
+        def row(table):
+            word = self.z * 0
+            for i in range(NZ):
+                word = word + (self.z == i).astype(jnp.int32) * table[i]
+            return word
+
+        return tuple(row(t) for t in (FROM_BELOW, FROM_ABOVE, FROM_BEFORE, TO_ABOVE, TO_BELOW))
+
+    def sends(self, t, words):
+        z = self.z
+        t = z * 0 + t
+        out = []
+        for link, (word, by) in enumerate(((words[3], 1), (words[4], NZ - 1))):
+            src = lax.rem(word, 32)
+            dst = jnp.where(src == OWN, z, src)
+            to = self.xy * NZ + lax.rem(z + by, NZ)
+            out.append((src != NONE, (jnp.minimum(src, OWN), jnp.minimum(dst, OWN - 1), link * ROUNDS + t, to)))
+        dst = lax.rem(words[2], 32)
+        earlier = jnp.where(dst == NZ + z, OWN, jnp.where(dst < NZ, dst + NZ, dst - NZ))
+        src = jnp.where(t == 1, OWN, earlier)
+        to = lax.rem(self.c + NZ * (1 + (t == 1).astype(jnp.int32)), NZ * NXY)
+        out.append((dst != NONE, (jnp.minimum(src, OWN), jnp.minimum(dst, OWN - 1), 2 * ROUNDS + t, to)))
+        return out
+
+    def start_round(self, t, words):
+        for condition, what in self.sends(t, words):
+            pl.when(condition)(lambda what=what: self.piece(*what).start())
+
+    def received(self, words):
+        return [lax.rem(word, 32) for word in words[:3]]
+
+    def take_round(self, words):
+        for slot in self.received(words):
+            pl.when(slot != NONE)(lambda slot=slot: self.arrived(slot))
+
+    @staticmethod
+    def following(words):
+        return tuple(word // 32 for word in words)
+
+    def finish(self, words):
+        def one(t, words):
+            for condition, what in self.sends(t, words):
+                pl.when(condition)(lambda what=what: self.piece(*what).wait_send())
+            return self.following(words)
+
+        lax.fori_loop(0, ROUNDS, one, words)
 
     def prompt_z(self, pk, pv):
         z = self.z
@@ -187,16 +177,18 @@
             rows = pl.ds(pl.multiple_of(source * 64, 64), 64)
             block = self.pg.at[self.role, rows]
             remote(block, block, self.ps.at[8 + s], self.pr.at[8 + s], self.c, self.r).wait_recv()
+        self.core_copy().start()
+
+    def core_copy(self):
         half = self.pg.at[self.role]
-        self.corecopy = remote(half, half, self.ps.at[0], self.pr.at[0], self.c, self.mate)
-        self.corecopy.start()
+        return remote(half, half, self.ps.at[0], self.pr.at[0], self.c, self.mate)
 
     def prompt_done(self):
         other = self.pg.at[1 - self.role]
         remote(other, other, self.ps.at[0], self.pr.at[0], self.c, self.mate).wait_recv()
 
     def prompt_sent(self):
-        for copy in self.zcopies + self.xycopies + [self.corecopy]:
+        for copy in self.zcopies + self.xycopies + [self.core_copy()]:
             copy.wait_send()
 
 
@@ -455,7 +447,7 @@
     pltpu.VMEM((17, T, 1024), jnp.bfloat16),
     pltpu.VMEM((2, PR, 512), jnp.bfloat16),
     pltpu.VMEM((NZ, 8, 512), jnp.float32),
-    pltpu.SemaphoreType.DMA((20,)),
+    pltpu.SemaphoreType.DMA((3 * ROUNDS,)),
     pltpu.SemaphoreType.DMA((16,)),
     pltpu.SemaphoreType.DMA((16,)),
     pltpu.SemaphoreType.DMA((16,)),
@@ -487,31 +479,37 @@
     g.prompt_z(pk, pv)
     loads[0].wait()
     loads[1].wait()
-    g.start_own()
+    words = g.tables()
+    g.start_round(0, words)
     loads[2].wait()
     loads[3].wait()
     a.prepare()
+    a.slot_block(OWN)
     g.prompt_xy()
-    g.take_first()
-    a.slot_block(OWN)
-    g.prompt_core()
-
-    @pl.loop(1, NZ + 1)
-    def _(s):
-        pl.when(s < NZ)(lambda: g.take_step(s))
-
-        @pl.loop(0, 4)
+
+    def one_round(t, words):
+        later = g.following(words)
+        g.take_round(words)
+        pl.when(t < ROUNDS)(lambda: g.start_round(t, later))
+        slots = g.received(words)
+
+        @pl.loop(0, 3)
         def _(i):
-            choices = [g.candidate(s - 1, j) for j in range(4)]
-            present, slot = choices[0][0], choices[0][1]
-            for j in range(1, 4):
-                present = jnp.where(i == j, choices[j][0].astype(jnp.int32), present.astype(jnp.int32))
-                slot = jnp.where(i == j, choices[j][1], slot)
-            pl.when(present > 0)(lambda: a.slot_block(slot))
-
-        pl.when(s == 2)(g.prompt_done)
-        pl.when((s > 2) & (s < 7))(lambda: a.prompt_block(s - 3))
-
+            slot = jnp.where(i == 0, slots[0], jnp.where(i == 1, slots[1], slots[2]))
+            pl.when(slot != NONE)(lambda: a.slot_block(slot))
+
+        pl.when(t == 2)(g.prompt_core)
+        pl.when(t == 3)(g.prompt_done)
+        low = jnp.minimum(jnp.maximum(t - 3, 0), 2) + 2 * (t // ROUNDS)
+        high = jnp.maximum(t - 2, 0) + t // 5 - t // ROUNDS
+
+        @pl.loop(0, 2)
+        def _(i):
+            pl.when(low + i < high)(lambda: a.prompt_block(low + i))
+
+        return later
+
+    lax.fori_loop(1, ROUNDS + 1, one_round, words)
     a.settle()
     a.prompt_grads(part)
     r.core_start()
@@ -532,7 +530,7 @@
     a.store(dq)
     r.finish()
     g.prompt_sent()
-    g.finish()
+    g.finish(words)
 
 
 VM = pl.BlockSpec(memory_space=pltpu.VMEM)

time: 117 us -> 99.3 us (0.85)
  the two profiles are of different devices: /device:TPU:153 before, /device:TPU:1 now
where the time goes in v3:
time: 99.3 us; the launch traced here: 99.1 us
  Pallas kernels  95.2 us (96%)
  local copies, waits for them, and re-layouts  3.27 us (3%)
    pallas_call x1, Pallas kernels, body(): pl.pallas_call(kernel, out_shape=(jax.ShapeDtypeStruct((T, HQ * D), jnp.b...  95.2 us
    unnamed x7, local copies, waits for them, and re-layouts  3.27 us

profile of v3, /device:TPU:1, one launch (start us, length us, event | category | flops | bytes accessed | tf_op | source)
XLA Modules:
  0.0 99.1 jit_solution(8611155928582976613)
XLA Ops:
  0.6 95.2 %shared_prompt_backward.1 = (bf16[128,2560]{1,0:T(8,128)(2,1)}, bf16[8,512]{1,0:T(8,128)(2,1)}, bf16[8,512]{1,0:T(8,128)(2,1)}) custom-call(bf16[128,2560]{1,0:T(8,128)(2,1)} %bitcast.5, bf16[128,2560]{1,0:T(8,128)(2,1)} %bitcast.6, bf16[128,512]{1,0:T(8,128)(2,1)} %bitcast.8, bf16[128,512]{1,0:T(8,128)(2,1)} %bitcast.9, bf16[8,512]{1,0:T(8,128)(2,1)} %pk.1, ...), custom_call_target="tpu_custom_call" | custom-call | tf_op jit(solution)/shard_map/shared_prompt_backward/pallas_call | solution.py:543
  95.8 0.0 copy-start.1
  95.8 2.0 %copy.13 = bf16[1,128,2560]{2,1,0:T(8,128)(2,1)} copy(bf16[1,128,2560]{2,1,0:T(8,128)(2,1)} %bitcast.7) | data formatting | bytes 1310720
  97.8 0.0 copy-done.1
  97.8 0.0 copy-start
  97.8 0.6 copy.14
  98.4 0.1 copy-done
  98.5 0.6 copy.15
Async XLA Ops:
  95.8 2.0 %copy-start.1 = (bf16[8,512]{1,0:T(8,128)(2,1)S(1)}, bf16[8,512]{1,0:T(8,128)(2,1)}, u32[]{:S(2)}) copy-start(bf16[8,512]{1,0:T(8,128)(2,1)} %get-tuple-element.13) | copy-start | bytes 24580
  97.8 0.7 copy-start

commit v4 on v3

--- a/solution.py
+++ b/solution.py
@@ -54,7 +54,7 @@
     barrier = pltpu.get_barrier_semaphore()
     for ctx, resp in peers:
         pl.semaphore_signal(barrier, inc=1, device_id=(ctx, resp), device_id_type=MESH)
-    pl.semaphore_wait(barrier, len(peers))
+    return barrier, len(peers)
 
 
 class Gather:
@@ -72,11 +72,18 @@
         out.append((self.c, self.mate))
         return out
 
-    def piece(self, src, dst, send, ctx):
-        return remote(self.kv.at[src], self.kv.at[dst], self.ks.at[send], self.kr.at[dst], ctx, self.r)
-
-    def arrived(self, slot):
-        self.piece(slot, slot, slot, self.c).wait_recv()
+    def piece(self, half, src, dst, send, ctx):
+        return remote(
+            self.kv.at[half, src],
+            self.kv.at[half, dst],
+            self.ks.at[half * 3 * ROUNDS + send],
+            self.kr.at[half * OWN + dst],
+            ctx,
+            self.r,
+        )
+
+    def arrived(self, half, slot):
+        self.piece(half, slot, slot, 0, self.c).wait_recv()
 
     @staticmethod
     def when(condition, do):
@@ -110,16 +117,16 @@
         out.append((dst != NONE, (jnp.minimum(src, OWN), jnp.minimum(dst, OWN - 1), 2 * ROUNDS + t, to)))
         return out
 
-    def start_round(self, t, words):
+    def start_round(self, half, t, words):
         for condition, what in self.sends(t, words):
-            pl.when(condition)(lambda what=what: self.piece(*what).start())
+            pl.when(condition)(lambda what=what: self.piece(half, *what).start())
 
     def received(self, words):
         return [lax.rem(word, 32) for word in words[:3]]
 
-    def take_round(self, words):
+    def take_round(self, half, words):
         for slot in self.received(words):
-            pl.when(slot != NONE)(lambda slot=slot: self.arrived(slot))
+            pl.when(slot != NONE)(lambda slot=slot: self.arrived(half, slot))
 
     @staticmethod
     def following(words):
@@ -128,7 +135,8 @@
     def finish(self, words):
         def one(t, words):
             for condition, what in self.sends(t, words):
-                pl.when(condition)(lambda what=what: self.piece(*what).wait_send())
+                for half in range(2):
+                    pl.when(condition)(lambda half=half, what=what: self.piece(half, *what).wait_send())
             return self.following(words)
 
         lax.fori_loop(0, ROUNDS, one, words)
@@ -151,33 +159,36 @@
         for copy in self.zcopies:
             copy.start()
 
-    def prompt_xy(self):
-        for s, copy in enumerate(self.zcopies, 1):
+    def prompt_pair(self):
+        for s in range(1, NZ):
             source = lax.rem(self.z - s + NZ, NZ)
             remote(self.za.at[source], self.za.at[source], self.ps.at[s], self.pr.at[s], self.c, self.r).wait_recv()
         rows = pl.ds(pl.multiple_of(self.xy * 64, 64), 64)
         self.pg[self.role, rows, :] = self.za[...].reshape(64, 512).astype(jnp.bfloat16)
-        self.xycopies = [
-            remote(
-                self.pg.at[self.role, rows],
-                self.pg.at[self.role, rows],
-                self.ps.at[8 + s],
-                self.pr.at[8 + s],
-                lax.rem(self.xy + s, NXY) * NZ + self.z,
-                self.r,
-            )
-            for s in range(1, NXY)
-        ]
-        for copy in self.xycopies:
-            copy.start()
-
-    def prompt_core(self):
-        for s in range(1, NXY):
-            source = lax.rem(self.xy - s + NXY, NXY)
-            rows = pl.ds(pl.multiple_of(source * 64, 64), 64)
-            block = self.pg.at[self.role, rows]
-            remote(block, block, self.ps.at[8 + s], self.pr.at[8 + s], self.c, self.r).wait_recv()
-        self.core_copy().start()
+        self.pair_copy(self.xy).start()
+
+    def pair_copy(self, xy):
+        block = self.pg.at[self.role, pl.ds(pl.multiple_of(xy * 64, 64), 64)]
+        to = self.xy + 1 - 2 * lax.rem(self.xy, 2)
+        return remote(block, block, self.ps.at[8], self.pr.at[8], to * NZ + self.z, self.r)
+
+    def x_copy(self, k):
+        x = lax.rem(self.xy // 2 + k, 4)
+        block = self.pg.at[self.role, pl.ds(pl.multiple_of(x * 128, 128), 128)]
+        to = lax.rem(self.c + 6 * NZ, NXY * NZ)
+        return remote(block, block, self.ps.at[9 + k], self.pr.at[9 + k], to, self.r)
+
+    def prompt_hop(self, k):
+        if k == 0:
+            self.pair_copy(self.xy + 1 - 2 * lax.rem(self.xy, 2)).wait_recv()
+        else:
+            x = lax.rem(self.xy // 2 + k, 4)
+            block = self.pg.at[self.role, pl.ds(pl.multiple_of(x * 128, 128), 128)]
+            remote(block, block, self.ps.at[8 + k], self.pr.at[8 + k], self.c, self.r).wait_recv()
+        if k < 3:
+            self.x_copy(k).start()
+        else:
+            self.core_copy().start()
 
     def core_copy(self):
         half = self.pg.at[self.role]
@@ -188,7 +199,7 @@
         remote(other, other, self.ps.at[0], self.pr.at[0], self.c, self.mate).wait_recv()
 
     def prompt_sent(self):
-        for copy in self.zcopies + self.xycopies + [self.core_copy()]:
+        for copy in self.zcopies + [self.pair_copy(self.xy)] + [self.x_copy(k) for k in range(3)] + [self.core_copy()]:
             copy.wait_send()
 
 
@@ -262,8 +273,8 @@
         bias = self.bias(slot)
         row = slot * T if isinstance(slot, int) else pl.multiple_of(slot * T, T)
         self.forward(
-            lambda k: self.kv[slot, :, pl.ds(pl.multiple_of(k * D, D), D)],
-            lambda k: self.kv[slot, :, pl.ds(pl.multiple_of(512 + k * D, D), D)],
+            lambda k: self.kv[0, slot, :, pl.ds(pl.multiple_of(k * D, D), D)],
+            lambda k: self.kv[1, slot, :, pl.ds(pl.multiple_of(k * D, D), D)],
             bias,
             row,
             slot,
@@ -297,19 +308,23 @@
     def add_dq(self, k, keys, ds):
         self.dq[k] += lax.dot_general(keys, ds, (((0,), (0,)), ((), ())), preferred_element_type=jnp.float32)
 
-    def prompt_grads(self, part):
+    def prompt_grads(self, part, ready):
         @pl.loop(0, KVH)
         def _(k):
             cols = pl.ds(pl.multiple_of(k * D, D), D)
-            blocks = []
             for i in range(4):
                 rows = slice(i * T, (i + 1) * T)
                 p, ds = self.grads(k, 17 + i, PROMPT + i * T, self.ep[k, rows, :])
-                blocks.append(ds)
+                self.ep[k, rows, :] = ds.astype(jnp.float32)
                 part[0, rows, cols] = jnp.dot(ds, self.qn[k], preferred_element_type=jnp.float32)
                 part[1, rows, cols] = jnp.dot(p.astype(jnp.bfloat16), self.don[k], preferred_element_type=jnp.float32)
-            ds = jnp.concatenate(blocks, axis=0)
-            self.add_dq(k, self.pg[0, :, cols], ds)
+            ready(k, cols)
+
+    def prompt_dq(self):
+        @pl.loop(0, KVH)
+        def _(k):
+            cols = pl.ds(pl.multiple_of(k * D, D), D)
+            self.add_dq(k, self.pg[0, :, cols], self.ep[k].astype(jnp.bfloat16))
 
     def slot_grads(self, slot):
         row = slot * T if isinstance(slot, int) else pl.multiple_of(slot * T, T)
@@ -317,7 +332,7 @@
         @pl.loop(0, KVH)
         def _(k):
             _, ds = self.grads(k, slot, row, self.slot_e(k, row))
-            self.add_dq(k, self.kv[slot, :, pl.ds(pl.multiple_of(k * D, D), D)], ds)
+            self.add_dq(k, self.kv[0, slot, :, pl.ds(pl.multiple_of(k * D, D), D)], ds)
 
     def pair_grads(self, pair):
         row = pl.multiple_of(pair * 2 * T, 2 * T)
@@ -327,7 +342,7 @@
             _, d0 = self.grads(k, 2 * pair, row, self.slot_e(k, row))
             _, d1 = self.grads(k, 2 * pair + 1, row + T, self.slot_e(k, row + T))
             cols = pl.ds(pl.multiple_of(k * D, D), D)
-            keys = self.kv[pl.ds(2 * pair, 2), :, cols].reshape(2 * T, D)
+            keys = self.kv[0, pl.ds(2 * pair, 2), :, cols].reshape(2 * T, D)
             self.add_dq(k, keys, jnp.concatenate([d0, d1], axis=0))
 
     def store(self, out):
@@ -356,14 +371,17 @@
 class Reduce:
     def __init__(self, part, ko, vo, sc):
         self.part, self.ko, self.vo = part, ko, vo
-        (self.s0, self.r0, self.acc, self.s1, self.r1, self.acc2, self.r2, self.s3, self.r3, self.ss, self.rs) = sc
+        (self.s0, self.r0, self.acc, self.s1, self.r1, self.acc2, self.r2, self.s3, self.r3) = sc[:9]
+        self.ss, self.rs, self.zs, self.zr = sc[9:]
         self.c, self.r, self.z, self.xy, self.role, self.mate = place()
         self.ylo = self.r // 2
+        self.other_y = (1 - self.ylo) * 2 + self.role
 
     def peers(self):
         out = [(self.c, self.mate)]
         for s in range(1, NZ):
-            out.append((self.xy * NZ + lax.rem(self.z + s, NZ), self.r))
+            ctx = self.xy * NZ + lax.rem(self.z + s, NZ)
+            out += [(ctx, self.r), (ctx, self.other_y)]
         for s in range(1, 16):
             out.append(self.target(s)[:2])
         return out
@@ -373,48 +391,72 @@
         other = lax.rem(me + s, 16)
         return (other // 2) * NZ + self.z, lax.rem(other, 2) * 2 + self.role, other
 
-    def core_start(self):
-        self.s0[...] = self.part[1 - self.role].astype(jnp.bfloat16)
-        self.first = remote(self.s0, self.r0, self.ss.at[0], self.rs.at[0], self.c, self.mate)
-        self.first.start()
-
-    def z_start(self):
-        z = self.z
-        self.first.wait_recv()
-        for i in range(NXY):
-            rows = slice(i * 64, (i + 1) * 64)
-            self.acc[i] = (self.part[self.role, rows, :] + self.r0[rows, :].astype(jnp.float32)).reshape(NZ, 8, 512)
-        for i in range(NZ):
-            self.s1[i] = self.acc[:, i].reshape(64, 512).astype(jnp.bfloat16)
+    def core_copy(self, k):
+        return remote(self.s0.at[k], self.r0.at[k], self.ss.at[k], self.rs.at[k], self.c, self.mate)
+
+    def core_start(self, k, cols):
+        self.s0[k] = self.part[1 - self.role, :, cols].astype(jnp.bfloat16)
+        self.core_copy(k).start()
+
+    def chip_start(self):
+        for k in range(KVH):
+            self.core_copy(k).wait_recv()
+            cols = slice(k * D, (k + 1) * D)
+            total = self.part[self.role, :, cols] + self.r0[k].astype(jnp.float32)
+            self.acc[:, cols] = total
+            self.s1[:, cols] = total.astype(jnp.bfloat16)
         self.copies = []
-        for s in range(1, NZ):
-            other = lax.rem(z + s, NZ)
-            self.copies.append(
-                remote(self.s1.at[other], self.r1.at[s], self.ss.at[s], self.rs.at[s], self.xy * NZ + other, self.r)
-            )
+        for s in range(1, 16):
+            ctx, resp, other = self.target(s)
+            rows = self.s1.at[pl.ds(pl.multiple_of(other * 32, 32), 32)]
+            self.copies.append(remote(rows, self.r1.at[s], self.ss.at[8 + s], self.rs.at[8 + s], ctx, resp))
         for copy in self.copies:
             copy.start()
 
-    def ring_start(self):
-        total = self.acc[:, self.z].reshape(64, 512)
+    def z_copies(self):
+        out = []
+        for q in range(4):
+            to = 4 * self.ylo + q
+            for b, resp in enumerate((self.r, self.other_y)):
+                copy = remote(
+                    self.acc2.at[q],
+                    self.r2.at[self.z],
+                    self.zs.at[2 * q + b],
+                    self.zr.at[self.z],
+                    self.xy * NZ + to,
+                    resp,
+                )
+                out.append((None if b else to != self.z, copy))
+        return out
+
+    def z_start(self):
+        me = self.xy * 2 + self.ylo
+        total = self.acc[pl.ds(pl.multiple_of(me * 32, 32), 32), :]
         for s, copy in enumerate(self.copies, 1):
             copy.wait_recv()
             total = total + self.r1[s].astype(jnp.float32)
-        self.acc2[...] = total.reshape(NXY, 8, 512)
-        self.second = []
-        for s in range(1, 16):
-            ctx, resp, other = self.target(s)
-            self.second.append(
-                remote(self.acc2.at[other // 2], self.r2.at[s], self.ss.at[8 + s], self.rs.at[8 + s], ctx, resp)
-            )
-        for copy in self.second:
-            copy.start()
+        self.acc2[...] = total.reshape(4, 8, 512)
+        for condition, copy in self.z_copies():
+            Gather.when(condition, copy.start)
 
     def mate_start(self):
-        total = self.acc2[self.xy]
-        for s, copy in enumerate(self.second, 1):
-            copy.wait_recv()
-            total = total + self.r2[s]
+        z = self.z
+        mine = z // 4 == self.ylo
+
+        @pl.when(mine)
+        def _():
+            self.r2[z] = self.acc2[lax.rem(z, 4)]
+
+        for i in range(NZ):
+
+            @pl.when(jnp.logical_not(mine & (z == i)))
+            def _(i=i):
+                slot = self.r2.at[i]
+                remote(slot, slot, self.zs.at[0], self.zr.at[i], self.c, self.r).wait_recv()
+
+        total = self.r2[0]
+        for i in range(1, NZ):
+            total = total + self.r2[i]
         self.s3[...] = total
         self.last = remote(self.s3, self.r3, self.ss.at[8], self.rs.at[8], self.c, self.mate)
         self.last.start()
@@ -424,31 +466,35 @@
         mine, other = self.s3[...], self.r3[...]
         self.ko[...] = jnp.where(self.role == 0, mine, other).astype(jnp.bfloat16)
         self.vo[...] = jnp.where(self.role == 0, other, mine).astype(jnp.bfloat16)
-        for copy in [self.first] + self.copies + self.second + [self.last]:
+        for copy in [self.core_copy(k) for k in range(KVH)] + self.copies + [self.last]:
             copy.wait_send()
+        for condition, copy in self.z_copies():
+            Gather.when(condition, copy.wait_send)
 
 
 REDUCE_SCRATCH = [
-    pltpu.VMEM((512, 512), jnp.bfloat16),
-    pltpu.VMEM((512, 512), jnp.bfloat16),
-    pltpu.VMEM((NXY, NZ, 8, 512), jnp.float32),
-    pltpu.VMEM((NZ, 64, 512), jnp.bfloat16),
-    pltpu.VMEM((NZ, 64, 512), jnp.bfloat16),
-    pltpu.VMEM((NXY, 8, 512), jnp.float32),
-    pltpu.VMEM((16, 8, 512), jnp.float32),
+    pltpu.VMEM((KVH, PR, D), jnp.bfloat16),
+    pltpu.VMEM((KVH, PR, D), jnp.bfloat16),
+    pltpu.VMEM((PR, 512), jnp.float32),
+    pltpu.VMEM((PR, 512), jnp.bfloat16),
+    pltpu.VMEM((16, 32, 512), jnp.bfloat16),
+    pltpu.VMEM((4, 8, 512), jnp.float32),
+    pltpu.VMEM((NZ, 8, 512), jnp.float32),
     pltpu.VMEM((8, 512), jnp.float32),
     pltpu.VMEM((8, 512), jnp.float32),
     pltpu.SemaphoreType.DMA((24,)),
     pltpu.SemaphoreType.DMA((24,)),
+    pltpu.SemaphoreType.DMA((8,)),
+    pltpu.SemaphoreType.DMA((8,)),
 ]
 
 
 GATHER_SCRATCH = [
-    pltpu.VMEM((17, T, 1024), jnp.bfloat16),
+    pltpu.VMEM((2, 17, T, 512), jnp.bfloat16),
     pltpu.VMEM((2, PR, 512), jnp.bfloat16),
     pltpu.VMEM((NZ, 8, 512), jnp.float32),
-    pltpu.SemaphoreType.DMA((3 * ROUNDS,)),
-    pltpu.SemaphoreType.DMA((16,)),
+    pltpu.SemaphoreType.DMA((6 * ROUNDS,)),
+    pltpu.SemaphoreType.DMA((2 * OWN,)),
     pltpu.SemaphoreType.DMA((16,)),
     pltpu.SemaphoreType.DMA((16,)),
 ]
@@ -468,29 +514,32 @@
     r = Reduce(part, ko, vo, scratch[ng + no + na :])
     a = Attend(q, do, g.kv, g.pg, lengths, scratch[ng + no : ng + no + na])
     loads = [
-        pltpu.make_async_copy(k_in, g.kv.at[OWN, :, pl.ds(0, 512)], sems.at[0]),
-        pltpu.make_async_copy(v_in, g.kv.at[OWN, :, pl.ds(512, 512)], sems.at[1]),
+        pltpu.make_async_copy(k_in, g.kv.at[0, OWN], sems.at[0]),
+        pltpu.make_async_copy(v_in, g.kv.at[1, OWN], sems.at[1]),
         pltpu.make_async_copy(q_in, q, sems.at[2]),
         pltpu.make_async_copy(do_in, do, sems.at[3]),
     ]
     for copy in loads:
         copy.start()
-    greet(r.peers())
+    barrier, arrivals = greet(r.peers())
+    for copy in loads:
+        copy.wait()
+    a.prepare()
+    pl.semaphore_wait(barrier, arrivals)
     g.prompt_z(pk, pv)
-    loads[0].wait()
-    loads[1].wait()
     words = g.tables()
-    g.start_round(0, words)
-    loads[2].wait()
-    loads[3].wait()
-    a.prepare()
+    g.start_round(0, 0, words)
+    g.start_round(1, 0, words)
+    g.prompt_pair()
     a.slot_block(OWN)
-    g.prompt_xy()
 
     def one_round(t, words):
         later = g.following(words)
-        g.take_round(words)
-        pl.when(t < ROUNDS)(lambda: g.start_round(t, later))
+        for half in range(2):
+            g.take_round(half, words)
+            pl.when(t < ROUNDS)(lambda half=half: g.start_round(half, t, later))
+        pl.when(t == 1)(lambda: g.prompt_hop(0))
+        pl.when(t == 2)(lambda: g.prompt_hop(2))
         slots = g.received(words)
 
         @pl.loop(0, 3)
@@ -498,7 +547,8 @@
             slot = jnp.where(i == 0, slots[0], jnp.where(i == 1, slots[1], slots[2]))
             pl.when(slot != NONE)(lambda: a.slot_block(slot))
 
-        pl.when(t == 2)(g.prompt_core)
+        pl.when(t == 1)(lambda: g.prompt_hop(1))
+        pl.when(t == 2)(lambda: g.prompt_hop(3))
         pl.when(t == 3)(g.prompt_done)
         low = jnp.minimum(jnp.maximum(t - 3, 0), 2) + 2 * (t // ROUNDS)
         high = jnp.maximum(t - 2, 0) + t // 5 - t // ROUNDS
@@ -511,16 +561,16 @@
 
     lax.fori_loop(1, ROUNDS + 1, one_round, words)
     a.settle()
-    a.prompt_grads(part)
-    r.core_start()
+    a.prompt_grads(part, r.core_start)
+    r.chip_start()
+    a.prompt_dq()
     a.slot_grads(OWN)
-    r.z_start()
 
     @pl.loop(0, 5)
     def _(pair):
         a.pair_grads(pair)
 
-    r.ring_start()
+    r.z_start()
 
     @pl.loop(5, 8)
     def _(pair):

time: 99.3 us -> 83.5 us (0.84)
  Pallas kernels: 95.2 us -> 79.3 us
    pallas_call x1, Pallas kernels: 95.2 us -> 79.3 us  [body(): pl.pallas_call(kernel, out_shape=(jax.ShapeDtypeStruct((T, HQ * D), jnp.b...]
where the time goes in v4:
time: 83.5 us; the launch traced here: 83.3 us
  Pallas kernels  79.3 us (95%)
  local copies, waits for them, and re-layouts  3.27 us (4%)
    pallas_call x1, Pallas kernels, body(): pl.pallas_call(kernel, out_shape=(jax.ShapeDtypeStruct((T, HQ * D), jnp.b...  79.3 us
    unnamed x7, local copies, waits for them, and re-layouts  3.27 us

profile of v4, /device:TPU:1, one launch (start us, length us, event | category | flops | bytes accessed | tf_op | source)
XLA Modules:
  0.0 83.3 jit_solution(7050205854519614542)
XLA Ops:
  0.6 79.3 %shared_prompt_backward.1 = (bf16[128,2560]{1,0:T(8,128)(2,1)}, bf16[8,512]{1,0:T(8,128)(2,1)}, bf16[8,512]{1,0:T(8,128)(2,1)}) custom-call(bf16[128,2560]{1,0:T(8,128)(2,1)} %bitcast.5, bf16[128,2560]{1,0:T(8,128)(2,1)} %bitcast.6, bf16[128,512]{1,0:T(8,128)(2,1)} %bitcast.8, bf16[128,512]{1,0:T(8,128)(2,1)} %bitcast.9, bf16[8,512]{1,0:T(8,128)(2,1)} %pk.1, ...), custom_call_target="tpu_custom_call" | custom-call | tf_op jit(solution)/shard_map/shared_prompt_backward/pallas_call | solution.py:593
  80.0 0.0 copy-start.1
  80.0 2.0 %copy.13 = bf16[1,128,2560]{2,1,0:T(8,128)(2,1)} copy(bf16[1,128,2560]{2,1,0:T(8,128)(2,1)} %bitcast.7) | data formatting | bytes 1310720
  81.9 0.0 copy-done.1
  82.0 0.0 copy-start
  82.0 0.6 copy.14
  82.6 0.1 copy-done
  82.7 0.6 copy.15
Async XLA Ops:
  80.0 2.0 %copy-start.1 = (bf16[8,512]{1,0:T(8,128)(2,1)S(1)}, bf16[8,512]{1,0:T(8,128)(2,1)}, u32[]{:S(2)}) copy-start(bf16[8,512]{1,0:T(8,128)(2,1)} %get-tuple-element.13) | copy-start | bytes 24580
  82.0 0.7 copy-start

commit v5 on v4

--- a/solution.py
+++ b/solution.py
@@ -246,7 +246,7 @@
         return jnp.where(visible, 0.0, NEG).astype(jnp.float32)
 
     def forward(self, keys, values, bias, row, block, n):
-        @pl.loop(0, KVH)
+        @pl.loop(0, KVH, unroll=True)
         def _(k):
             s = jnp.dot(keys(k), self.qt[k], preferred_element_type=jnp.float32)
             dp = jnp.dot(values(k), self.dot_[k], preferred_element_type=jnp.float32)
@@ -371,17 +371,17 @@
 class Reduce:
     def __init__(self, part, ko, vo, sc):
         self.part, self.ko, self.vo = part, ko, vo
-        (self.s0, self.r0, self.acc, self.s1, self.r1, self.acc2, self.r2, self.s3, self.r3) = sc[:9]
-        self.ss, self.rs, self.zs, self.zr = sc[9:]
+        (self.s0, self.r0, self.acc, self.s1, self.r1, self.acc2, self.r2, self.res) = sc[:8]
+        self.ss, self.rs, self.zs, self.zr = sc[8:]
         self.c, self.r, self.z, self.xy, self.role, self.mate = place()
         self.ylo = self.r // 2
         self.other_y = (1 - self.ylo) * 2 + self.role
+        self.far = (1 - self.ylo) * 2 + 1 - self.role
 
     def peers(self):
-        out = [(self.c, self.mate)]
+        out = [(self.c, self.mate), (self.c, self.far)]
         for s in range(1, NZ):
-            ctx = self.xy * NZ + lax.rem(self.z + s, NZ)
-            out += [(ctx, self.r), (ctx, self.other_y)]
+            out.append((self.xy * NZ + lax.rem(self.z + s, NZ), self.r))
         for s in range(1, 16):
             out.append(self.target(s)[:2])
         return out
@@ -417,16 +417,10 @@
         out = []
         for q in range(4):
             to = 4 * self.ylo + q
-            for b, resp in enumerate((self.r, self.other_y)):
-                copy = remote(
-                    self.acc2.at[q],
-                    self.r2.at[self.z],
-                    self.zs.at[2 * q + b],
-                    self.zr.at[self.z],
-                    self.xy * NZ + to,
-                    resp,
-                )
-                out.append((None if b else to != self.z, copy))
+            copy = remote(
+                self.acc2.at[q], self.r2.at[self.z], self.zs.at[q], self.zr.at[self.z], self.xy * NZ + to, self.r
+            )
+            out.append((to != self.z, copy))
         return out
 
     def z_start(self):
@@ -439,37 +433,54 @@
         for condition, copy in self.z_copies():
             Gather.when(condition, copy.start)
 
-    def mate_start(self):
+    def out_copies(self):
+        block = self.res.at[self.role]
+        places = (self.mate, self.other_y, self.far)
+        return [
+            remote(block, block, self.zs.at[4 + i], self.rs.at[4 + self.role], self.c, resp)
+            for i, resp in enumerate(places)
+        ]
+
+    def owners_start(self):
         z = self.z
-        mine = z // 4 == self.ylo
-
-        @pl.when(mine)
+
+        @pl.when(z // 4 == self.ylo)
         def _():
             self.r2[z] = self.acc2[lax.rem(z, 4)]
-
-        for i in range(NZ):
-
-            @pl.when(jnp.logical_not(mine & (z == i)))
+            for i in range(NZ):
+
+                @pl.when(z != i)
+                def _(i=i):
+                    slot = self.r2.at[i]
+                    remote(slot, slot, self.zs.at[0], self.zr.at[i], self.c, self.r).wait_recv()
+
+            total = self.r2[0]
+            for i in range(1, NZ):
+                total = total + self.r2[i]
+            self.res[self.role] = total
+            for copy in self.out_copies():
+                copy.start()
+
+    def finish(self):
+        owner = self.z // 4 == self.ylo
+        for i in range(2):
+
+            @pl.when(jnp.logical_not(owner & (self.role == i)))
             def _(i=i):
-                slot = self.r2.at[i]
-                remote(slot, slot, self.zs.at[0], self.zr.at[i], self.c, self.r).wait_recv()
-
-        total = self.r2[0]
-        for i in range(1, NZ):
-            total = total + self.r2[i]
-        self.s3[...] = total
-        self.last = remote(self.s3, self.r3, self.ss.at[8], self.rs.at[8], self.c, self.mate)
-        self.last.start()
-
-    def finish(self):
-        self.last.wait_recv()
-        mine, other = self.s3[...], self.r3[...]
-        self.ko[...] = jnp.where(self.role == 0, mine, other).astype(jnp.bfloat16)
-        self.vo[...] = jnp.where(self.role == 0, other, mine).astype(jnp.bfloat16)
-        for copy in [self.core_copy(k) for k in range(KVH)] + self.copies + [self.last]:
+                block = self.res.at[i]
+                remote(block, block, self.zs.at[0], self.rs.at[4 + i], self.c, self.mate).wait_recv()
+
+        self.ko[...] = self.res[0].astype(jnp.bfloat16)
+        self.vo[...] = self.res[1].astype(jnp.bfloat16)
+        for copy in [self.core_copy(k) for k in range(KVH)] + self.copies:
             copy.wait_send()
         for condition, copy in self.z_copies():
             Gather.when(condition, copy.wait_send)
+
+        @pl.when(owner)
+        def _():
+            for copy in self.out_copies():
+                copy.wait_send()
 
 
 REDUCE_SCRATCH = [
@@ -480,8 +491,7 @@
     pltpu.VMEM((16, 32, 512), jnp.bfloat16),
     pltpu.VMEM((4, 8, 512), jnp.float32),
     pltpu.VMEM((NZ, 8, 512), jnp.float32),
-    pltpu.VMEM((8, 512), jnp.float32),
-    pltpu.VMEM((8, 512), jnp.float32),
+    pltpu.VMEM((2, 8, 512), jnp.float32),
     pltpu.SemaphoreType.DMA((24,)),
     pltpu.SemaphoreType.DMA((24,)),
     pltpu.SemaphoreType.DMA((8,)),
@@ -539,7 +549,7 @@
             g.take_round(half, words)
             pl.when(t < ROUNDS)(lambda half=half: g.start_round(half, t, later))
         pl.when(t == 1)(lambda: g.prompt_hop(0))
-        pl.when(t == 2)(lambda: g.prompt_hop(2))
+        pl.when(t == 3)(lambda: g.prompt_hop(3))
         slots = g.received(words)
 
         @pl.loop(0, 3)
@@ -548,10 +558,10 @@
             pl.when(slot != NONE)(lambda: a.slot_block(slot))
 
         pl.when(t == 1)(lambda: g.prompt_hop(1))
-        pl.when(t == 2)(lambda: g.prompt_hop(3))
+        pl.when(t == 2)(lambda: g.prompt_hop(2))
         pl.when(t == 3)(g.prompt_done)
-        low = jnp.minimum(jnp.maximum(t - 3, 0), 2) + 2 * (t // ROUNDS)
-        high = jnp.maximum(t - 2, 0) + t // 5 - t // ROUNDS
+        low = 1 * (t > 3).astype(jnp.int32) + 2 * (t > 4).astype(jnp.int32) + 1 * (t > 5).astype(jnp.int32)
+        high = 1 * (t >= 3).astype(jnp.int32) + 2 * (t >= 4).astype(jnp.int32) + 1 * (t >= 5).astype(jnp.int32)
 
         @pl.loop(0, 2)
         def _(i):
@@ -576,7 +586,7 @@
     def _(pair):
         a.pair_grads(pair)
 
-    r.mate_start()
+    r.owners_start()
     a.store(dq)
     r.finish()
     g.prompt_sent()

time: 83.5 us -> 79.8 us (0.956)
  Pallas kernels: 79.3 us -> 75.4 us
    pallas_call x1, Pallas kernels: 79.3 us -> 75.4 us  [body(): pl.pallas_call(kernel, out_shape=(jax.ShapeDtypeStruct((T, HQ * D), jnp.b...]
where the time goes in v5:
time: 79.8 us; the launch traced here: 79.3 us
  Pallas kernels  75.4 us (94%)
  local copies, waits for them, and re-layouts  3.27 us (4%)
    pallas_call x1, Pallas kernels, body(): pl.pallas_call(kernel, out_shape=(jax.ShapeDtypeStruct((T, HQ * D), jnp.b...  75.4 us
    unnamed x7, local copies, waits for them, and re-layouts  3.27 us

profile of v5, /device:TPU:1, one launch (start us, length us, event | category | flops | bytes accessed | tf_op | source)
XLA Modules:
  0.0 79.3 jit_solution(2506409843919140861)
XLA Ops:
  0.6 75.4 %shared_prompt_backward.1 = (bf16[128,2560]{1,0:T(8,128)(2,1)}, bf16[8,512]{1,0:T(8,128)(2,1)}, bf16[8,512]{1,0:T(8,128)(2,1)}) custom-call(bf16[128,2560]{1,0:T(8,128)(2,1)} %bitcast.5, bf16[128,2560]{1,0:T(8,128)(2,1)} %bitcast.6, bf16[128,512]{1,0:T(8,128)(2,1)} %bitcast.8, bf16[128,512]{1,0:T(8,128)(2,1)} %bitcast.9, bf16[8,512]{1,0:T(8,128)(2,1)} %pk.1, ...), custom_call_target="tpu_custom_call" | custom-call | tf_op jit(solution)/shard_map/shared_prompt_backward/pallas_call | solution.py:603
  76.0 0.0 copy-start.1
  76.1 2.0 %copy.13 = bf16[1,128,2560]{2,1,0:T(8,128)(2,1)} copy(bf16[1,128,2560]{2,1,0:T(8,128)(2,1)} %bitcast.7) | data formatting | bytes 1310720
  78.0 0.0 copy-done.1
  78.0 0.0 copy-start
  78.0 0.6 copy.14
  78.6 0.1 copy-done
  78.7 0.6 copy.15
Async XLA Ops:
  76.0 2.0 %copy-start.1 = (bf16[8,512]{1,0:T(8,128)(2,1)S(1)}, bf16[8,512]{1,0:T(8,128)(2,1)}, u32[]{:S(2)}) copy-start(bf16[8,512]{1,0:T(8,128)(2,1)} %get-tuple-element.13) | copy-start | bytes 24580
  78.0 0.7 copy-start

commit v6 on v5

--- a/solution.py
+++ b/solution.py
@@ -309,7 +309,7 @@
         self.dq[k] += lax.dot_general(keys, ds, (((0,), (0,)), ((), ())), preferred_element_type=jnp.float32)
 
     def prompt_grads(self, part, ready):
-        @pl.loop(0, KVH)
+        @pl.loop(0, KVH, unroll=True)
         def _(k):
             cols = pl.ds(pl.multiple_of(k * D, D), D)
             for i in range(4):

time: 79.8 us -> 80 us (level)
  no operation moved by 1% of the time
where the time goes in v6:
time: 80 us; the launch traced here: 79.6 us
  Pallas kernels  75.7 us (95%)
  local copies, waits for them, and re-layouts  3.27 us (4%)
    pallas_call x1, Pallas kernels, body(): pl.pallas_call(kernel, out_shape=(jax.ShapeDtypeStruct((T, HQ * D), jnp.b...  75.7 us
    unnamed x7, local copies, waits for them, and re-layouts  3.27 us

profile of v6, /device:TPU:1, one launch (start us, length us, event | category | flops | bytes accessed | tf_op | source)
XLA Modules:
  0.0 79.6 jit_solution(8427581942040553135)
XLA Ops:
  0.6 75.7 %shared_prompt_backward.1 = (bf16[128,2560]{1,0:T(8,128)(2,1)}, bf16[8,512]{1,0:T(8,128)(2,1)}, bf16[8,512]{1,0:T(8,128)(2,1)}) custom-call(bf16[128,2560]{1,0:T(8,128)(2,1)} %bitcast.5, bf16[128,2560]{1,0:T(8,128)(2,1)} %bitcast.6, bf16[128,512]{1,0:T(8,128)(2,1)} %bitcast.8, bf16[128,512]{1,0:T(8,128)(2,1)} %bitcast.9, bf16[8,512]{1,0:T(8,128)(2,1)} %pk.1, ...), custom_call_target="tpu_custom_call" | custom-call | tf_op jit(solution)/shard_map/shared_prompt_backward/pallas_call | solution.py:603
  76.3 0.0 copy-start.1
  76.3 2.0 %copy.13 = bf16[1,128,2560]{2,1,0:T(8,128)(2,1)} copy(bf16[1,128,2560]{2,1,0:T(8,128)(2,1)} %bitcast.7) | data formatting | bytes 1310720
  78.3 0.0 copy-done.1
  78.3 0.0 copy-start
  78.3 0.6 copy.14
  78.9 0.1 copy-done
  79.0 0.6 copy.15
Async XLA Ops:
  76.3 2.0 %copy-start.1 = (bf16[8,512]{1,0:T(8,128)(2,1)S(1)}, bf16[8,512]{1,0:T(8,128)(2,1)}, u32[]{:S(2)}) copy-start(bf16[8,512]{1,0:T(8,128)(2,1)} %get-tuple-element.13) | copy-start | bytes 24580
  78.3 0.7 copy-start
